TPU v7x, 32 devices: a whole 2x2x4 slice. The times are simulated.
32 devices in a mesh: dp: 4 (over y, x), fsdp: 8 (over z, core).
Axes of the slice: x: 2, y: 2, z: 4, core: 2. Of those that a mesh axis runs over, the one named last changes fastest.
Arguments:
- inputs: bfloat16 [8, 512, 2048], P('dp', 'fsdp'), may hold values from -11.2 to 11.2
- block_ids: int32 [8, 512], P('dp'), may hold values from 0 to 3, never falling along the last dimension, each value on 1 to 256 neighbouring positions
- cotangent: bfloat16 [8, 512, 2048], P('dp', 'fsdp'), may hold values from -6 to 6
- ln1_gain: bfloat16 [2048], P(('dp', 'fsdp')), may hold values from 0.25 to 1.75
- ln1_bias: bfloat16 [2048], P(('dp', 'fsdp')), may hold values from -1.5 to 1.5
- query_weight: bfloat16 [2048, 2048], P(('dp', 'fsdp')), may hold values from -0.25 to 0.25
- query_bias: bfloat16 [2048], P(('dp', 'fsdp')), may hold values from -1.5 to 1.5
- key_weight: bfloat16 [2048, 2048], P(('dp', 'fsdp')), may hold values from -0.125 to 0.125
- value_weight: bfloat16 [2048, 2048], P(('dp', 'fsdp')), may hold values from -0.125 to 0.125
- value_bias: bfloat16 [2048], P(('dp', 'fsdp')), may hold values from -1.5 to 1.5
- out_weight: bfloat16 [2048, 2048], P(('dp', 'fsdp')), may hold values from -0.5 to 0.5
- out_bias: bfloat16 [2048], P(('dp', 'fsdp')), may hold values from -1.5 to 1.5
- ln2_gain: bfloat16 [2048], P(('dp', 'fsdp')), may hold values from 0.25 to 1.75
- ln2_bias: bfloat16 [2048], P(('dp', 'fsdp')), may hold values from -1.5 to 1.5
- up_weight: bfloat16 [2048, 8192], P(('dp', 'fsdp')), may hold values from -0.125 to 0.125
- up_bias: bfloat16 [8192], P(('dp', 'fsdp')), may hold values from -1.5 to 1.5
- down_weight: bfloat16 [8192, 2048], P(('dp', 'fsdp')), may hold values from -0.09375 to 0.09375
- down_bias: bfloat16 [2048], P(('dp', 'fsdp')), may hold values from -1.5 to 1.5
Outputs:
- output: bfloat16 [8, 512, 2048], P('dp', 'fsdp')
- input_grad: float32 [8, 512, 2048], P('dp', 'fsdp')
- ln1_gain_grad: float32 [2048], P(('dp', 'fsdp'))
- ln1_bias_grad: float32 [2048], P(('dp', 'fsdp'))
- query_weight_grad: float32 [2048, 2048], P(('dp', 'fsdp'))
- query_bias_grad: float32 [2048], P(('dp', 'fsdp'))
- key_weight_grad: float32 [2048, 2048], P(('dp', 'fsdp'))
- value_weight_grad: float32 [2048, 2048], P(('dp', 'fsdp'))
- value_bias_grad: float32 [2048], P(('dp', 'fsdp'))
- out_weight_grad: float32 [2048, 2048], P(('dp', 'fsdp'))
- out_bias_grad: float32 [2048], P(('dp', 'fsdp'))
- ln2_gain_grad: float32 [2048], P(('dp', 'fsdp'))
- ln2_bias_grad: float32 [2048], P(('dp', 'fsdp'))
- up_weight_grad: float32 [2048, 8192], P(('dp', 'fsdp'))
- up_bias_grad: float32 [8192], P(('dp', 'fsdp'))
- down_weight_grad: float32 [8192, 2048], P(('dp', 'fsdp'))
- down_bias_grad: float32 [2048], P(('dp', 'fsdp'))
- rms_input: float32 [], replicated
- rms_attention: float32 [], replicated
- rms_mlp: float32 [], replicated
Inputs may be any that keep to these rules, and one draw needn't show every extreme that they name: `block_ids`: block ids never fall along a sequence; positions with one id form one attention block of 1 to 256 positions.
All inputs are finite; a program needn't handle non-finite values.
Results may differ from a plain program's by a relative error of at most 0.018.
Values may be sent and summed in bfloat16 or wider, within the bound.
No kernel may reach another device: no remote copies, remote signals or barrier semaphores. Data moves between devices by JAX's collectives and lax.ppermute only.
A program may use at most 448 MiB of HBM per device.

v0:
```python
from functools import partial
import math

import jax
import jax.numpy as jnp
from jax import lax
from jax.sharding import PartitionSpec as P

HEADS = 16
HEAD = 128


EPSILON = 1e-05
NEGATIVE = -1e30


def layer_norm(values, gain, shift):
    center = values - jnp.mean(values, axis=-1, keepdims=True)
    spread = jnp.mean(center * center, axis=-1, keepdims=True)
    return center * lax.rsqrt(spread + EPSILON) * gain + shift


def product(left, right):
    return jnp.dot(left, right, preferred_element_type=jnp.float32)


def product_left_t(left, right):
    return lax.dot_general(
        left, right, (((0,), (0,)), ((), ())), preferred_element_type=jnp.float32
    )


def product_right_t(left, right):
    return lax.dot_general(
        left, right, (((1,), (1,)), ((), ())), preferred_element_type=jnp.float32
    )


def masked_scores(query_part, key_part, allowed):
    scores = jnp.einsum("qhe,khe->hqk", query_part, key_part, preferred_element_type=jnp.float32)
    return jnp.where(allowed[None], scores, NEGATIVE)


def attend_forward(query_part, key_part, value_part, allowed):
    scores = masked_scores(query_part, key_part, allowed)
    peak = jnp.max(scores, axis=-1, keepdims=True)
    expo = jnp.exp(scores - peak)
    total = jnp.sum(expo, axis=-1, keepdims=True)
    probs = (expo / total).astype(jnp.bfloat16)
    mixed = jnp.einsum("hqk,khe->qhe", probs, value_part, preferred_element_type=jnp.float32)
    return (mixed, peak + jnp.log(total))


def attend_backward(query_part, key_part, value_part, allowed, log_total, grad_part):
    scores = masked_scores(query_part, key_part, allowed)
    probs = jnp.exp(scores - log_total)
    probs_low = probs.astype(jnp.bfloat16)
    grad_probs = jnp.einsum(
        "qhe,khe->hqk", grad_part, value_part, preferred_element_type=jnp.float32
    )
    delta = jnp.sum(probs * grad_probs, axis=-1, keepdims=True)
    grad_scores = (probs * (grad_probs - delta)).astype(jnp.bfloat16)
    grad_query = jnp.einsum(
        "hqk,khe->qhe", grad_scores, key_part, preferred_element_type=jnp.float32
    )
    grad_key = jnp.einsum(
        "hqk,qhe->khe", grad_scores, query_part, preferred_element_type=jnp.float32
    )
    grad_value = jnp.einsum(
        "hqk,qhe->khe", probs_low, grad_part, preferred_element_type=jnp.float32
    )
    return (grad_query, grad_key, grad_value)


def add_shards(totals, latest):
    if totals is None:
        return latest
    return tuple((left + right for left, right in zip(totals, latest)))


def local(
    inputs,
    block_ids,
    cotangent,
    ln1_gain,
    ln1_bias,
    query_weight,
    query_bias,
    key_weight,
    value_weight,
    value_bias,
    out_weight,
    out_bias,
    ln2_gain,
    ln2_bias,
    up_weight,
    up_bias,
    down_weight,
    down_bias,
):
    micro, rows, width = inputs.shape
    scale = 1.0 / math.sqrt(HEAD)
    group = 2
    own = lax.axis_index("fsdp")
    input_square = jnp.zeros((), jnp.float32)
    branch_square = jnp.zeros((), jnp.float32)
    mlp_square = jnp.zeros((), jnp.float32)
    (
        gain_one,
        bias_one,
        query_full,
        query_shift,
        key_full,
        value_full,
        value_shift,
        out_full,
        out_shift,
    ) = (
        lax.all_gather(ln1_gain, ("dp", "fsdp"), axis=0, tiled=True),
        lax.all_gather(ln1_bias, ("dp", "fsdp"), axis=0, tiled=True),
        lax.all_gather(query_weight, ("dp", "fsdp"), axis=0, tiled=True),
        lax.all_gather(query_bias, ("dp", "fsdp"), axis=0, tiled=True),
        lax.all_gather(key_weight, ("dp", "fsdp"), axis=0, tiled=True),
        lax.all_gather(value_weight, ("dp", "fsdp"), axis=0, tiled=True),
        lax.all_gather(value_bias, ("dp", "fsdp"), axis=0, tiled=True),
        lax.all_gather(out_weight, ("dp", "fsdp"), axis=0, tiled=True),
        lax.all_gather(out_bias, ("dp", "fsdp"), axis=0, tiled=True),
    )
    gain_two, bias_two, up_full, up_shift, down_full, down_shift = (
        lax.all_gather(ln2_gain, ("dp", "fsdp"), axis=0, tiled=True),
        lax.all_gather(ln2_bias, ("dp", "fsdp"), axis=0, tiled=True),
        lax.all_gather(up_weight, ("dp", "fsdp"), axis=0, tiled=True),
        lax.all_gather(up_bias, ("dp", "fsdp"), axis=0, tiled=True),
        lax.all_gather(down_weight, ("dp", "fsdp"), axis=0, tiled=True),
        lax.all_gather(down_bias, ("dp", "fsdp"), axis=0, tiled=True),
    )
    gain_one_f = gain_one.astype(jnp.float32)
    bias_one_f = bias_one.astype(jnp.float32)
    gain_two_f = gain_two.astype(jnp.float32)
    bias_two_f = bias_two.astype(jnp.float32)
    kept_forward = []
    output_rows = []
    for micro_index in range(micro):
        tokens = inputs[micro_index].astype(jnp.float32)
        block_row = block_ids[micro_index]
        input_square = input_square + jnp.sum(tokens * tokens)
        normed_low = layer_norm(tokens, gain_one_f, bias_one_f).astype(jnp.bfloat16)
        queries = (
            (product(normed_low, query_full) + query_shift.astype(jnp.float32)) * scale
        ).astype(jnp.bfloat16)
        keys = product(normed_low, key_full).astype(jnp.bfloat16)
        values = (product(normed_low, value_full) + value_shift.astype(jnp.float32)).astype(
            jnp.bfloat16
        )
        key_all, value_all = (
            lax.all_gather(keys, "fsdp", axis=0, tiled=True),
            lax.all_gather(values, "fsdp", axis=0, tiled=True),
        )
        length = key_all.shape[0]
        query_ids = lax.dynamic_slice_in_dim(block_row, own * rows, rows, 0)
        allowed = block_row[None, :] <= query_ids[:, None]
        query_heads = queries.reshape(rows, HEADS, HEAD)
        key_heads = key_all.reshape(length, HEADS, HEAD)
        value_heads = value_all.reshape(length, HEADS, HEAD)
        mixed_parts = []
        log_parts = []
        for first in range(0, HEADS, group):
            mixed, log_total = attend_forward(
                query_heads[:, first : first + group],
                key_heads[:, first : first + group],
                value_heads[:, first : first + group],
                allowed,
            )
            mixed_parts.append(mixed)
            log_parts.append(log_total)
        attended = jnp.concatenate(mixed_parts, axis=1).reshape(rows, width).astype(jnp.bfloat16)
        softmax_saved = (allowed, log_parts)
        branch = product(attended, out_full) + out_shift.astype(jnp.float32)
        hidden_in = tokens + branch
        normed_two_low = layer_norm(hidden_in, gain_two_f, bias_two_f).astype(jnp.bfloat16)
        pre_act = product(normed_two_low, up_full) + up_shift.astype(jnp.float32)
        activation = jax.nn.gelu(pre_act, approximate=False).astype(jnp.bfloat16)
        branch_two = product(activation, down_full) + down_shift.astype(jnp.float32)
        output_full = hidden_in + branch_two
        output_rows.append(output_full.astype(jnp.bfloat16))
        branch_square = branch_square + jnp.sum(branch * branch)
        mlp_square = mlp_square + jnp.sum(output_full * output_full)
        kept_forward.append(
            (
                tokens,
                block_row,
                normed_low,
                query_heads,
                key_heads,
                value_heads,
                softmax_saved,
                attended,
                hidden_in,
                normed_two_low,
                pre_act,
                activation,
            )
        )
    input_total, branch_total, mlp_total = lax.psum(
        (input_square, branch_square, mlp_square), ("dp", "fsdp")
    )
    mlp_totals = None
    hidden_grads = []
    for micro_index in range(micro):
        (
            tokens,
            block_row,
            normed_low,
            query_heads,
            key_heads,
            value_heads,
            softmax_saved,
            attended,
            hidden_in,
            normed_two_low,
            pre_act,
            activation,
        ) = kept_forward[micro_index]
        grad_out = cotangent[micro_index]
        grad_float = grad_out.astype(jnp.float32)
        down_grad = product_left_t(activation, grad_out)
        down_bias_grad = jnp.sum(grad_float, axis=0)
        grad_act = product_right_t(grad_out, down_full)
        gelu_value, gelu_pull = jax.vjp(partial(jax.nn.gelu, approximate=False), pre_act)
        grad_pre = gelu_pull(grad_act)[0].astype(jnp.bfloat16)
        up_grad = product_left_t(normed_two_low, grad_pre)
        up_bias_grad = jnp.sum(grad_pre.astype(jnp.float32), axis=0)
        grad_normed_two = product_right_t(grad_pre, up_full)
        norm_value, norm_pull = jax.vjp(layer_norm, hidden_in, gain_two_f, bias_two_f)
        grad_hidden, gain_two_grad, bias_two_grad = norm_pull(grad_normed_two)
        hidden_grads.append(grad_hidden + grad_float)
        mlp_totals = add_shards(
            mlp_totals,
            (gain_two_grad, bias_two_grad, up_grad, up_bias_grad, down_grad, down_bias_grad),
        )
    mlp_shards = lax.psum_scatter(mlp_totals, ("dp", "fsdp"), scatter_dimension=0, tiled=True)
    attn_totals = None
    grad_rows = []
    for micro_index in range(micro):
        (
            tokens,
            block_row,
            normed_low,
            query_heads,
            key_heads,
            value_heads,
            softmax_saved,
            attended,
            hidden_in,
            normed_two_low,
            pre_act,
            activation,
        ) = kept_forward[micro_index]
        grad_hidden = hidden_grads[micro_index]
        grad_branch = grad_hidden.astype(jnp.bfloat16)
        out_grad = product_left_t(attended, grad_branch)
        out_bias_grad = jnp.sum(grad_branch.astype(jnp.float32), axis=0)
        grad_attended = product_right_t(grad_branch, out_full).astype(jnp.bfloat16)
        allowed, log_parts = softmax_saved
        length = key_heads.shape[0]
        grad_heads_rows = grad_attended.reshape(rows, HEADS, HEAD)
        query_parts = []
        key_parts = []
        value_parts = []
        for group_index, first in enumerate(range(0, HEADS, group)):
            grad_query, grad_key, grad_value = attend_backward(
                query_heads[:, first : first + group],
                key_heads[:, first : first + group],
                value_heads[:, first : first + group],
                allowed,
                log_parts[group_index],
                grad_heads_rows[:, first : first + group],
            )
            key_own, value_own = (
                lax.psum_scatter(
                    grad_key.reshape(length, group * HEAD).astype(jnp.bfloat16),
                    "fsdp",
                    scatter_dimension=0,
                    tiled=True,
                ).astype(jnp.float32),
                lax.psum_scatter(
                    grad_value.reshape(length, group * HEAD).astype(jnp.bfloat16),
                    "fsdp",
                    scatter_dimension=0,
                    tiled=True,
                ).astype(jnp.float32),
            )
            query_parts.append(grad_query.reshape(rows, group * HEAD))
            key_parts.append(key_own.astype(jnp.bfloat16))
            value_parts.append(value_own.astype(jnp.bfloat16))
        grad_query_low = jnp.concatenate(query_parts, axis=1).astype(jnp.bfloat16)
        grad_key_low = jnp.concatenate(key_parts, axis=1)
        grad_value_low = jnp.concatenate(value_parts, axis=1)
        query_grad = product_left_t(normed_low, grad_query_low) * scale
        query_bias_grad = jnp.sum(grad_query_low.astype(jnp.float32), axis=0) * scale
        key_grad = product_left_t(normed_low, grad_key_low)
        value_grad = product_left_t(normed_low, grad_value_low)
        value_bias_grad = jnp.sum(grad_value_low.astype(jnp.float32), axis=0)
        grad_normed = (
            product_right_t(grad_query_low, query_full) * scale
            + product_right_t(grad_key_low, key_full)
            + product_right_t(grad_value_low, value_full)
        )
        first_value, first_pull = jax.vjp(layer_norm, tokens, gain_one_f, bias_one_f)
        grad_tokens, gain_one_grad, bias_one_grad = first_pull(grad_normed)
        grad_rows.append(grad_hidden + grad_tokens)
        attn_totals = add_shards(
            attn_totals,
            (
                gain_one_grad,
                bias_one_grad,
                query_grad,
                query_bias_grad,
                key_grad,
                value_grad,
                value_bias_grad,
                out_grad,
                out_bias_grad,
            ),
        )
    attn_shards = lax.psum_scatter(attn_totals, ("dp", "fsdp"), scatter_dimension=0, tiled=True)
    entries = micro * rows * lax.axis_size(("dp", "fsdp")) * width
    rms_input = jnp.sqrt(input_total / entries)
    rms_attention = jnp.sqrt(branch_total / entries)
    rms_mlp = jnp.sqrt(mlp_total / entries)
    output = jnp.stack(output_rows, axis=0)
    input_grad = jnp.stack(grad_rows, axis=0)
    (
        gain_one_sum,
        bias_one_sum,
        query_sum,
        query_bias_sum,
        key_sum,
        value_sum,
        value_bias_sum,
        out_sum,
        out_bias_sum,
    ) = attn_shards
    gain_two_sum, bias_two_sum, up_sum, up_bias_sum, down_sum, down_bias_sum = mlp_shards
    return (
        output,
        input_grad,
        gain_one_sum,
        bias_one_sum,
        query_sum,
        query_bias_sum,
        key_sum,
        value_sum,
        value_bias_sum,
        out_sum,
        out_bias_sum,
        gain_two_sum,
        bias_two_sum,
        up_sum,
        up_bias_sum,
        down_sum,
        down_bias_sum,
        rms_input,
        rms_attention,
        rms_mlp,
    )


def solution(mesh):
    in_specs = (
        P("dp", "fsdp", None),
        P("dp", None),
        P("dp", "fsdp", None),
        P(("dp", "fsdp")),
        P(("dp", "fsdp")),
        P(("dp", "fsdp"), None),
        P(("dp", "fsdp")),
        P(("dp", "fsdp"), None),
        P(("dp", "fsdp"), None),
        P(("dp", "fsdp")),
        P(("dp", "fsdp"), None),
        P(("dp", "fsdp")),
        P(("dp", "fsdp")),
        P(("dp", "fsdp")),
        P(("dp", "fsdp"), None),
        P(("dp", "fsdp")),
        P(("dp", "fsdp"), None),
        P(("dp", "fsdp")),
    )
    out_specs = (
        P("dp", "fsdp", None),
        P("dp", "fsdp", None),
        P(("dp", "fsdp")),
        P(("dp", "fsdp")),
        P(("dp", "fsdp"), None),
        P(("dp", "fsdp")),
        P(("dp", "fsdp"), None),
        P(("dp", "fsdp"), None),
        P(("dp", "fsdp")),
        P(("dp", "fsdp"), None),
        P(("dp", "fsdp")),
        P(("dp", "fsdp")),
        P(("dp", "fsdp")),
        P(("dp", "fsdp"), None),
        P(("dp", "fsdp")),
        P(("dp", "fsdp"), None),
        P(("dp", "fsdp")),
        P(),
        P(),
        P(),
    )
    return jax.shard_map(local, mesh=mesh, in_specs=in_specs, out_specs=out_specs, check_vma=False)
```

profile of v0, /device:TPU:0, one launch (start us, length us, event | category | flops | bytes accessed | tf_op | source)
XLA Modules:
  0.0 4100.3 jit_solution(18005470834580112085)
XLA Ops:
  16.3 43.0 %all-reduce.18 = (bf16[2048]{0:T(1024)(128)(2,1)S(1)}, bf16[2048]{0:T(1024)(128)(2,1)S(1)}, bf16[2048]{0:T(1024)(128)(2,1)S(1)}, bf16[2048]{0:T(1024)(128)(2,1)S...) all-reduce(bf16[2048]{0:T(1024)(128)(2,1)S(1)} %dynamic-update-slic, ...), channel_id=1, replica_groups=mesh['dp'=4,'fsdp'=8] {'dp','fsdp'}, use_global_device_ids=true, to_apply=%add.4 | all-reduce | flops 16384 | bytes 65536
  62.0 29.4 all-gather.12.cloned.1.call-done
  103.0 67.6 %all-gather.18.cloned.1.call-done = bf16[2048,2048]{1,0:T(8,128)(2,1)} async-done(((bf16[64,2048]{1,0:T(8,128)(2,1)}), bf16[2048,2048]{1,0:T(8,128)(2,1)}) %all-gather.18.cloned.1.call-update) | async-done | bytes 8388624 | tf_op jit(solution)/shard_map/all_gather | solution.py:123
  184.9 39.4 all-gather
  224.6 25.0 all-gather.16.cloned.1.call-done
  258.9 20.5 all-gather.28.cloned.1.call-done
  281.6 28.4 all-gather.14.cloned.1.call-done
  313.6 27.1 all-gather.30.cloned.1.call-done
  344.3 27.3 all-gather.20.cloned.1.call-done
  423.5 27.9 all-gather.22.cloned.1.call-done
  460.7 187.1 %all-gather.24.cloned.1.call-done = bf16[2048,8192]{1,0:T(8,128)(2,1)} async-done(((bf16[64,8192]{1,0:T(8,128)(2,1)}), bf16[2048,8192]{1,0:T(8,128)(2,1)}) %all-gather.24.cloned.1.call-update) | async-done | bytes 33554448 | tf_op jit(solution)/shard_map/all_gather | solution.py:132
  663.7 180.1 %all-gather.26.cloned.1.call-done = bf16[8192,2048]{1,0:T(8,128)(2,1)} async-done(((bf16[256,2048]{1,0:T(8,128)(2,1)}), bf16[8192,2048]{1,0:T(8,128)(2,1)}) %all-gather.26.cloned.1.call-update) | async-done | bytes 33554448 | tf_op jit(solution)/shard_map/all_gather | solution.py:134
  893.0 20.2 convert_reduce_fusion.1
  1122.1 29.7 reduce-scatter.143.cloned.1.call-done
  1152.7 29.9 reduce-scatter.145.cloned.1.call-done
  1183.5 29.9 reduce-scatter.163.cloned.1.call-done
  1214.2 29.9 reduce-scatter.165.cloned.1.call-done
  1245.0 29.9 reduce-scatter.167.cloned.1.call-done
  1275.7 29.9 reduce-scatter.169.cloned.1.call-done
  1306.5 29.9 reduce-scatter.171.cloned.1.call-done
  1337.3 29.9 reduce-scatter.173.cloned.1.call-done
  1368.0 29.9 reduce-scatter.175.cloned.1.call-done
  1398.7 29.8 reduce-scatter.177.cloned.1.call-done
  1460.6 30.6 reduce-scatter.117.cloned.1.call-done
  1492.0 29.8 reduce-scatter.119.cloned.1.call-done
  1522.7 29.9 reduce-scatter.121.cloned.1.call-done
  1553.4 29.9 reduce-scatter.123.cloned.1.call-done
  1584.2 30.0 reduce-scatter.125.cloned.1.call-done
  1615.0 29.7 reduce-scatter.127.cloned.1.call-done
  1645.6 30.0 reduce-scatter.129.cloned.1.call-done
  1676.4 29.8 reduce-scatter.147.cloned.1.call-done
  1707.1 29.7 reduce-scatter.149.cloned.1.call-done
  1737.7 29.7 reduce-scatter.151.cloned.1.call-done
  1768.3 30.0 reduce-scatter.153.cloned.1.call-done
  1799.1 29.7 reduce-scatter.155.cloned.1.call-done
  1829.8 30.0 reduce-scatter.157.cloned.1.call-done
  1860.6 29.8 reduce-scatter.159.cloned.1.call-done
  1891.3 30.0 reduce-scatter.161.cloned.1.call-done
  1935.8 24.8 fusion.114
  1960.6 47.9 %convolution_add_fusion = f32[8192,2048]{1,0:T(8,128)} fusion(f32[8192,2048]{1,0:T(8,128)} %fusion.114, bf16[2,64,2048]{2,1,0:T(8,128)(2,1)S(1)} %copy-done.54, f32[64,8192]{1,0:T(8,128)} %convolution_add_fusion.2), kind=kOutput, calls=%fused_computation | convolution fusion | flops 2198339584 | bytes 136577024 | tf_op jit(solution)/shard_map/dot_general | solution.py:28
  2010.0 24.0 fusion.374
  2034.0 47.2 %convolution_add_fusion.1 = f32[2048,8192]{1,0:T(8,128)} fusion(f32[2048,8192]{1,0:T(8,128)} %fusion.374, bf16[64,8192]{1,0:T(8,128)(2,1)S(1)} %copy-done.50, f32[64,2048]{1,0:T(8,128)S(1)} %copy-done.5, f32[64]{0:T(128)S(1)} %copy-done.215, f32[64]{0:T(128)S(1)} %copy-done.211, f32[2048]{0:T(1024)S(1)} %copy-done.112, f32[2048]{0:T(1024)S(1)} %copy-done.110), kind=kOutput, calls=%fused_computation.1 | convolution fusion | flops 2164916224 | bytes 135807488 | tf_op jit(solution)/shard_map/dot_general | solution.py:28
  2146.1 41.5 %all-reduce.20 = (f32[2048]{0:T(1024)S(1)}, f32[2048]{0:T(1024)S(1)}, f32[2048]{0:T(1024)S(1)}, f32[2048]{0:T(1024)S(1)}, f32[2048]{0:T(1024)S(1)}, /*index=5*/f...) all-reduce(f32[2048]{0:T(1024)S(1)} %add.518, ...), channel_id=34, replica_groups=mesh['dp'=4,'fsdp'=8] {'dp','fsdp'}, use_global_device_ids=true, to_apply=%region_98.99.clone | all-reduce | flops 24579 | bytes 196632
  2196.7 100.5 %reduce-scatter.103.cloned.1.call-done = f32[64,2048]{1,0:T(8,128)} async-done(((f32[2048,2048]{1,0:T(8,128)}), f32[64,2048]{1,0:T(8,128)}) %reduce-scatter.103.cloned.1.call-update) | async-done | bytes 524304 | tf_op jit(solution)/shard_map/reduce_scatter | solution.py:326
  2297.1 187.1 %reduce-scatter.107.cloned.1.call-done = f32[64,2048]{1,0:T(8,128)} async-done(((f32[2048,2048]{1,0:T(8,128)}), f32[64,2048]{1,0:T(8,128)}) %reduce-scatter.107.cloned.1.call-update) | async-done | bytes 524304 | tf_op jit(solution)/shard_map/reduce_scatter | solution.py:326
  2484.3 187.1 %reduce-scatter.105.cloned.1.call-done = f32[64,2048]{1,0:T(8,128)} async-done(((f32[2048,2048]{1,0:T(8,128)}), f32[64,2048]{1,0:T(8,128)}) %reduce-scatter.105.cloned.1.call-update) | async-done | bytes 524304 | tf_op jit(solution)/shard_map/reduce_scatter | solution.py:326
  2671.3 709.9 %reduce-scatter.113.cloned.1.call-done = f32[256,2048]{1,0:T(8,128)} async-done(((f32[8192,2048]{1,0:T(8,128)}), f32[256,2048]{1,0:T(8,128)}) %reduce-scatter.113.cloned.1.call-update) | async-done | bytes 2097168 | tf_op jit(solution)/shard_map/reduce_scatter | solution.py:241
  3381.2 708.7 %reduce-scatter.111.cloned.1.call-done = f32[64,8192]{1,0:T(8,128)} async-done(((f32[2048,8192]{1,0:T(8,128)}), f32[64,8192]{1,0:T(8,128)}) %reduce-scatter.111.cloned.1.call-update) | async-done | bytes 2097168 | tf_op jit(solution)/shard_map/reduce_scatter | solution.py:241
  (1050 shorter events, 522.6 us)
Async XLA Ops:
  7.2 84.2 %all-gather.12.cloned.1.call-start = ((), (), s32[]{:S(2)}) async-start(), calls=%async_computation.38 | async-start | bytes 8650752 | tf_op jit(solution)/shard_map/all_gather | solution.py:124
  7.9 162.7 %all-gather.18.cloned.1.call-start = ((), (), s32[]{:S(2)}) async-start(), calls=%async_computation.41 | async-start | bytes 8650752 | tf_op jit(solution)/shard_map/all_gather | solution.py:123
  8.7 241.0 %all-gather.16.cloned.1.call-start = ((), (), s32[]{:S(2)}) async-start(), calls=%async_computation.40 | async-start | bytes 8650752 | tf_op jit(solution)/shard_map/all_gather | solution.py:121
  9.4 270.0 %all-gather.28.cloned.1.call-start = ((), (), s32[]{:S(2)}) async-start(), calls=%async_computation.46 | async-start | bytes 2359296 | tf_op jit(solution)/shard_map/all_gather | solution.py:157
  97.1 212.9 %all-gather.14.cloned.1.call-start = ((), (), s32[]{:S(2)}) async-start(), calls=%async_computation.39 | async-start | bytes 2359296 | tf_op jit(solution)/shard_map/all_gather | solution.py:157
  103.0 237.7 %all-gather.30.cloned.1.call-start = ((), (), s32[]{:S(2)}) async-start(), calls=%async_computation.47 | async-start | bytes 2359296 | tf_op jit(solution)/shard_map/all_gather | solution.py:156
  176.3 195.2 %all-gather.20.cloned.1.call-start = ((), (), s32[]{:S(2)}) async-start(), calls=%async_computation.42 | async-start | bytes 2359296 | tf_op jit(solution)/shard_map/all_gather | solution.py:156
  182.1 269.3 %all-gather.22.cloned.1.call-start = ((), (), s32[]{:S(2)}) async-start(), calls=%async_computation.43 | async-start | bytes 8650752 | tf_op jit(solution)/shard_map/all_gather | solution.py:126
  182.9 464.9 %all-gather.24.cloned.1.call-start = ((), (), s32[]{:S(2)}) async-start(), calls=%async_computation.44 | async-start | bytes 34603008 | tf_op jit(solution)/shard_map/all_gather | solution.py:132
  183.6 660.1 %all-gather.26.cloned.1.call-start = ((), (), s32[]{:S(2)}) async-start(), calls=%async_computation.45 | async-start | bytes 34603008 | tf_op jit(solution)/shard_map/all_gather | solution.py:134
  184.2 925.2 %reduce-scatter.131.cloned.1.call-start = ((), (), s32[]{:S(2)}) async-start(), calls=%async_computation.62 | async-start | bytes 294912
  938.8 171.4 %reduce-scatter.133.cloned.1.call-start = ((), (), s32[]{:S(2)}) async-start(), calls=%async_computation.63 | async-start | bytes 294912
  940.8 170.4 %reduce-scatter.135.cloned.1.call-start = ((), (), s32[]{:S(2)}) async-start(), calls=%async_computation.64 | async-start | bytes 294912
  942.8 169.3 %reduce-scatter.137.cloned.1.call-start = ((), (), s32[]{:S(2)}) async-start(), calls=%async_computation.65 | async-start | bytes 294912
  944.8 168.2 %reduce-scatter.139.cloned.1.call-start = ((), (), s32[]{:S(2)}) async-start(), calls=%async_computation.66 | async-start | bytes 294912
  946.7 174.5 %reduce-scatter.141.cloned.1.call-start = ((), (), s32[]{:S(2)}) async-start(), calls=%async_computation.67 | async-start | bytes 294912
  948.6 203.2 %reduce-scatter.143.cloned.1.call-start = ((), (), s32[]{:S(2)}) async-start(), calls=%async_computation.68 | async-start | bytes 294912
  950.6 232.0 %reduce-scatter.145.cloned.1.call-start = ((), (), s32[]{:S(2)}) async-start(), calls=%async_computation.69 | async-start | bytes 294912
  952.5 260.8 %reduce-scatter.163.cloned.1.call-start = ((), (), s32[]{:S(2)}) async-start(), calls=%async_computation.78 | async-start | bytes 294912
  961.4 282.6 %reduce-scatter.165.cloned.1.call-start = ((), (), s32[]{:S(2)}) async-start(), calls=%async_computation.79 | async-start | bytes 294912
  965.8 309.0 %reduce-scatter.167.cloned.1.call-start = ((), (), s32[]{:S(2)}) async-start(), calls=%async_computation.80 | async-start | bytes 294912
  970.1 335.5 %reduce-scatter.169.cloned.1.call-start = ((), (), s32[]{:S(2)}) async-start(), calls=%async_computation.81 | async-start | bytes 294912
  975.0 361.4 %reduce-scatter.171.cloned.1.call-start = ((), (), s32[]{:S(2)}) async-start(), calls=%async_computation.82 | async-start | bytes 294912
  978.6 388.5 %reduce-scatter.173.cloned.1.call-start = ((), (), s32[]{:S(2)}) async-start(), calls=%async_computation.83 | async-start | bytes 294912
  982.2 415.7 %reduce-scatter.175.cloned.1.call-start = ((), (), s32[]{:S(2)}) async-start(), calls=%async_computation.84 | async-start | bytes 294912
  986.4 442.2 %reduce-scatter.177.cloned.1.call-start = ((), (), s32[]{:S(2)}) async-start(), calls=%async_computation.85 | async-start | bytes 294912
  993.2 466.5 %reduce-scatter.115.cloned.1.call-start = ((), (), s32[]{:S(2)}) async-start(), calls=%async_computation.54 | async-start | bytes 294912
  1001.7 489.4 %reduce-scatter.117.cloned.1.call-start = ((), (), s32[]{:S(2)}) async-start(), calls=%async_computation.55 | async-start | bytes 294912
  1009.7 512.1 %reduce-scatter.119.cloned.1.call-start = ((), (), s32[]{:S(2)}) async-start(), calls=%async_computation.56 | async-start | bytes 294912
  1017.3 535.3 %reduce-scatter.121.cloned.1.call-start = ((), (), s32[]{:S(2)}) async-start(), calls=%async_computation.57 | async-start | bytes 294912
  1024.7 558.6 %reduce-scatter.123.cloned.1.call-start = ((), (), s32[]{:S(2)}) async-start(), calls=%async_computation.58 | async-start | bytes 294912
  1032.1 582.0 %reduce-scatter.125.cloned.1.call-start = ((), (), s32[]{:S(2)}) async-start(), calls=%async_computation.59 | async-start | bytes 294912
  1037.3 607.4 %reduce-scatter.127.cloned.1.call-start = ((), (), s32[]{:S(2)}) async-start(), calls=%async_computation.60 | async-start | bytes 294912
  1043.3 632.2 %reduce-scatter.129.cloned.1.call-start = ((), (), s32[]{:S(2)}) async-start(), calls=%async_computation.61 | async-start | bytes 294912
  1048.2 658.1 %reduce-scatter.147.cloned.1.call-start = ((), (), s32[]{:S(2)}) async-start(), calls=%async_computation.70 | async-start | bytes 294912
  1051.7 685.2 %reduce-scatter.149.cloned.1.call-start = ((), (), s32[]{:S(2)}) async-start(), calls=%async_computation.71 | async-start | bytes 294912
  1056.5 710.9 %reduce-scatter.151.cloned.1.call-start = ((), (), s32[]{:S(2)}) async-start(), calls=%async_computation.72 | async-start | bytes 294912
  1058.2 740.1 %reduce-scatter.153.cloned.1.call-start = ((), (), s32[]{:S(2)}) async-start(), calls=%async_computation.73 | async-start | bytes 294912
  1059.9 769.0 %reduce-scatter.155.cloned.1.call-start = ((), (), s32[]{:S(2)}) async-start(), calls=%async_computation.74 | async-start | bytes 294912
  1061.6 798.1 %reduce-scatter.157.cloned.1.call-start = ((), (), s32[]{:S(2)}) async-start(), calls=%async_computation.75 | async-start | bytes 294912
  1063.3 827.1 %reduce-scatter.159.cloned.1.call-start = ((), (), s32[]{:S(2)}) async-start(), calls=%async_computation.76 | async-start | bytes 294912
  1065.8 855.5 %reduce-scatter.161.cloned.1.call-start = ((), (), s32[]{:S(2)}) async-start(), calls=%async_computation.77 | async-start | bytes 294912
  1074.1 1122.6 %reduce-scatter.109.cloned.1.call-start = ((), (), s32[]{:S(2)}) async-start(), calls=%async_computation.51 | async-start | bytes 17301504 | tf_op jit(solution)/shard_map/reduce_scatter | solution.py:326
  1088.3 1208.9 %reduce-scatter.103.cloned.1.call-start = ((), (), s32[]{:S(2)}) async-start(), calls=%async_computation.48 | async-start | bytes 17301504 | tf_op jit(solution)/shard_map/reduce_scatter | solution.py:326
  1109.3 1375.0 %reduce-scatter.107.cloned.1.call-start = ((), (), s32[]{:S(2)}) async-start(), calls=%async_computation.50 | async-start | bytes 17301504 | tf_op jit(solution)/shard_map/reduce_scatter | solution.py:326
  1441.4 1229.9 %reduce-scatter.105.cloned.1.call-start = ((), (), s32[]{:S(2)}) async-start(), calls=%async_computation.49 | async-start | bytes 17301504 | tf_op jit(solution)/shard_map/reduce_scatter | solution.py:326
  1934.2 1447.0 %reduce-scatter.113.cloned.1.call-start = ((), (), s32[]{:S(2)}) async-start(), calls=%async_computation.53 | async-start | bytes 69206016 | tf_op jit(solution)/shard_map/reduce_scatter | solution.py:241
  2008.7 2081.3 %reduce-scatter.111.cloned.1.call-start = ((), (), s32[]{:S(2)}) async-start(), calls=%async_computation.52 | async-start | bytes 69206016 | tf_op jit(solution)/shard_map/reduce_scatter | solution.py:241
  (282 other events, 9728.5 us)
Sparse Core Ops, SparseCore 0:
  11.0 80.3 all-gather.11
  94.4 76.1 all-gather.17
  173.6 76.0 all-gather.15
  251.7 27.6 all-gather.27
  281.4 28.5 all-gather.13
  312.1 28.5 all-gather.29
  342.9 28.5 all-gather.19
  374.5 76.8 all-gather.21
  454.4 193.4 all-gather.23
  650.7 193.0 all-gather.25
  939.0 28.5 reduce-scatter.130
  969.7 28.5 reduce-scatter.132
  1000.6 28.5 reduce-scatter.134
  1031.3 28.4 reduce-scatter.136
  1062.0 28.4 reduce-scatter.138
  1092.6 28.5 reduce-scatter.140
  1123.3 28.4 reduce-scatter.142
  1154.0 28.5 reduce-scatter.144
  1184.8 28.4 reduce-scatter.162
  1215.5 28.4 reduce-scatter.164
  1246.3 28.4 reduce-scatter.166
  1277.1 28.4 reduce-scatter.168
  1307.9 28.4 reduce-scatter.170
  1338.6 28.4 reduce-scatter.172
  1369.4 28.4 reduce-scatter.174
  1400.1 28.4 reduce-scatter.176
  1431.2 28.4 reduce-scatter.114
  1462.6 28.4 reduce-scatter.116
  1493.4 28.4 reduce-scatter.118
  1524.0 28.5 reduce-scatter.120
  1554.8 28.4 reduce-scatter.122
  1585.6 28.4 reduce-scatter.124
  1616.2 28.4 reduce-scatter.126
  1647.0 28.4 reduce-scatter.128
  1677.8 28.4 reduce-scatter.146
  1708.4 28.3 reduce-scatter.148
  1738.9 28.4 reduce-scatter.150
  1769.8 28.4 reduce-scatter.152
  1800.4 28.4 reduce-scatter.154
  1831.2 28.4 reduce-scatter.156
  1862.0 28.4 reduce-scatter.158
  1892.7 28.4 reduce-scatter.160
  1924.0 184.7 reduce-scatter.108
  2111.7 185.4 reduce-scatter.102
  2299.9 184.3 reduce-scatter.106
  2487.0 184.3 reduce-scatter.104
  2674.1 707.0 reduce-scatter.112
  3384.0 705.8 reduce-scatter.110
where the time goes:
time: 4110 us; the launch traced here: 4100 us
  waiting for transfers between devices  3290 us (80%)
  matrix products  492 us (12%)
  blocking collectives  124 us (3%)
  local copies, waits for them, and re-layouts  111 us (3%)
  other arithmetic  49.8 us (1%)
    reduce_scatter x2, waiting for transfers between devices, local(): lax.psum_scatter(mlp_totals, ('dp', 'fsdp'), scatter_dimension=0, tiled=T...  1420 us
    unnamed x80, waiting for transfers between devices  778 us
    reduce_scatter x4, waiting for transfers between devices, local(): lax.psum_scatter(attn_totals, ('dp', 'fsdp'), scatter_dimension=0, tiled=...  475 us
    dot_general x12, matrix products, product_left_t(): lax.dot_general(left, right, (((0,), (0,)), ((), ())), preferred_element_...  198 us
    all_gather x1, waiting for transfers between devices, local(): lax.all_gather(up_weight, ('dp', 'fsdp'), axis=0, tiled=True)  187 us
    all_gather x1, waiting for transfers between devices, local(): lax.all_gather(down_weight, ('dp', 'fsdp'), axis=0, tiled=True)  180 us
    dot_general x12, matrix products, product_right_t(): lax.dot_general(left, right, (((1,), (1,)), ((), ())), preferred_element_...  108 us
    unnamed x704, local copies, waits for them, and re-layouts  102 us
  transfers between devices with their start and end apart: 48, of which 42 were waited for; matrix products, arithmetic and copies ran while one was open for 13% of the time, Pallas kernels for 0%

commit v1 on v0

v1 whole, which is shorter than its diff:
```python
import math

import jax
import jax.numpy as jnp
from jax import lax
from jax.sharding import PartitionSpec as P

HEAD = 128
EPSILON = 1e-05
NEGATIVE = -1e30
F32 = jnp.float32
BF16 = jnp.bfloat16


def dot(left, right, dims):
    return lax.dot_general(left, right, (dims, ((), ())), preferred_element_type=F32)


def mm(left, right):
    return dot(left, right, ((1,), (0,)))


def mm_lt(left, right):
    return dot(left, right, ((0,), (0,)))


def mm_rt(left, right):
    return dot(left, right, ((1,), (1,)))


def normalize(values):
    center = values - jnp.mean(values, axis=-1, keepdims=True)
    spread = jnp.mean(center * center, axis=-1, keepdims=True)
    inverse = lax.rsqrt(spread + EPSILON)
    return center * inverse, inverse


def normalize_back(normal, inverse, upstream):
    first = jnp.mean(upstream, axis=-1, keepdims=True)
    second = jnp.mean(upstream * normal, axis=-1, keepdims=True)
    return (upstream - first - normal * second) * inverse


def gelu_pair(values):
    half = 0.5 * (1.0 + lax.erf(values * (1.0 / math.sqrt(2.0))))
    density = jnp.exp(-0.5 * values * values) * (1.0 / math.sqrt(2.0 * math.pi))
    return values * half, half + values * density


def core_swap(array):
    size = lax.axis_size("fsdp")
    return lax.ppermute(array, "fsdp", [(f, f ^ 1) for f in range(size)])


def along_chips(array, pairs):
    return lax.ppermute(array, "fsdp", [(2 * a + c, 2 * b + c) for a, b in pairs for c in (0, 1)])


def turned(amount, chips):
    return [(i, (i + amount) % chips) for i in range(chips)]


def roll_first(array, shift):
    size = array.shape[0]
    return lax.dynamic_slice_in_dim(jnp.concatenate([array, array], axis=0), shift, size, 0)


class Line:
    def __init__(self):
        self.size = lax.axis_size("fsdp")
        self.chips = self.size // 2
        self.own = lax.axis_index("fsdp")
        self.chip = self.own // 2
        self.core = self.own % 2
        self.special = self.chips == 4

    def order(self, row):
        if not self.special:
            return row
        parts = row.reshape(self.chips, 2, -1)
        parts = roll_first(parts, self.chip)
        parts = jnp.where(self.core == 0, parts, parts[:, ::-1])
        return parts.transpose(1, 0, 2).reshape(row.shape)

    def gather(self, own):
        if not self.special:
            return lax.all_gather(own, "fsdp", axis=0, tiled=True)
        below = along_chips(own, turned(1, 4))
        above = along_chips(own, turned(3, 4))
        up = along_chips(below, [(1, 2), (2, 3)])
        down = along_chips(above, [(1, 0), (2, 1)])
        far = jnp.where(self.chip >= 2, up, down)
        mine = jnp.concatenate([own, above, far, below], axis=0)
        return jnp.concatenate([mine, core_swap(mine)], axis=0)

    def scatter(self, partial):
        if not self.special:
            whole = partial(slice(None)).astype(BF16)
            return lax.psum_scatter(whole, "fsdp", scatter_dimension=0, tiled=True).astype(F32)
        total = self.size * self.rows
        half = total // 2
        other = partial(slice(half, total)).astype(BF16)
        arrived = core_swap(other)
        mine = partial(slice(0, half)) + arrived.astype(F32)
        rows = self.rows
        own, next_up, far, next_down = (mine[i * rows : (i + 1) * rows] for i in range(4))
        far = far.astype(BF16)
        up = along_chips(far, [(0, 1), (1, 2)])
        down = along_chips(far, [(2, 1), (3, 2)])
        send_up = (next_up + up.astype(F32)).astype(BF16)
        send_down = (next_down + down.astype(F32)).astype(BF16)
        from_below = along_chips(send_up, turned(1, 4))
        from_above = along_chips(send_down, turned(3, 4))
        return own + from_below.astype(F32) + from_above.astype(F32)

    def exchange(self, blocks):
        chips = self.chips
        shape = blocks.shape[1:]
        pairs = roll_first(blocks.reshape((chips, 2) + shape), self.chip)
        arrived = [pairs[0]]
        for step in range(1, chips):
            arrived.append(along_chips(pairs[step], turned(step, chips)))
        stacked = jnp.stack([arrived[0]] + arrived[:0:-1], axis=0)
        keep = lax.dynamic_index_in_dim(stacked, self.core, 1, keepdims=False)
        give = lax.dynamic_index_in_dim(stacked, 1 - self.core, 1, keepdims=False)
        got = core_swap(give)
        both = jnp.where(self.core == 0, jnp.stack([keep, got], 1), jnp.stack([got, keep], 1))
        natural = roll_first(both, (chips - self.chip) % chips)
        return natural.reshape((self.size,) + shape)


def swap_bit(array, axis, bit):
    size = lax.axis_size(axis)
    return lax.ppermute(array, axis, [(i, i ^ bit) for i in range(size)])


def bits(axis):
    size = lax.axis_size(axis)
    return [1 << k for k in range(size.bit_length() - 1)]


def gather_small(own):
    held = own[None]
    for axis in ("fsdp", "dp"):
        index = lax.axis_index(axis)
        for bit in bits(axis):
            got = swap_bit(held, axis, bit)
            high = (index & bit) != 0
            held = jnp.where(
                high, jnp.concatenate([got, held], 0), jnp.concatenate([held, got], 0)
            )
    return held


def sum_small(values):
    for axis in ("dp", "fsdp"):
        for bit in bits(axis):
            values = values + swap_bit(values, axis, bit)
    return values


def local(
    inputs,
    block_ids,
    cotangent,
    ln1_gain,
    ln1_bias,
    query_weight,
    query_bias,
    key_weight,
    value_weight,
    value_bias,
    out_weight,
    out_bias,
    ln2_gain,
    ln2_bias,
    up_weight,
    up_bias,
    down_weight,
    down_bias,
):
    micro, rows, width = inputs.shape
    scale = 1.0 / math.sqrt(HEAD)
    groups = lax.axis_size("dp")
    size = lax.axis_size("fsdp")
    devices = groups * size
    line = Line()
    line.rows = rows
    dp_own = lax.axis_index("dp")
    own = line.own
    slab = width // devices
    span = HEAD // slab
    bands = size // span
    held = groups // span
    band, place = own // span, own % span
    hidden_slab = up_bias.shape[0]
    cols = held * HEAD

    vector = jnp.concatenate(
        [ln1_gain, ln1_bias, query_bias, value_bias, out_bias, ln2_gain, ln2_bias, down_bias, up_bias]
    )
    vectors = gather_small(vector)
    (gain_one, bias_one, query_shift, value_shift, out_shift, gain_two, bias_two, down_shift) = (
        vectors[:, i * slab : (i + 1) * slab].reshape(width).astype(F32) for i in range(8)
    )
    up_shift = vectors[:, 8 * slab :].reshape(groups, size, hidden_slab)
    up_shift = lax.dynamic_index_in_dim(up_shift, own, 1, keepdims=False).reshape(-1).astype(F32)

    def head_columns(row):
        split = row.reshape(span, held, bands, HEAD)
        split = lax.dynamic_index_in_dim(split, place, 0, keepdims=False)
        return lax.dynamic_index_in_dim(split, band, 1, keepdims=False).reshape(cols)

    def head_place(part):
        whole = jnp.zeros((span, held, bands, HEAD), F32)
        part = part.reshape(1, held, 1, HEAD)
        return lax.dynamic_update_slice(whole, part, (place, 0, band, 0)).reshape(width)

    query_shift = head_columns(query_shift)
    value_shift = head_columns(value_shift)

    qkv = jnp.stack([query_weight, key_weight, value_weight], axis=1)
    qkv = qkv.reshape(slab, 3, span, held, bands, HEAD).transpose(4, 2, 0, 1, 3, 5)
    qkv = line.exchange(qkv.reshape(size, slab, 3 * cols))
    qkv_full = lax.all_gather(qkv.reshape(size * slab, 3 * cols), "dp", axis=0, tiled=True)
    tokens_full = [line.gather(inputs[m]) for m in range(micro)]
    out_rows = lax.all_gather(out_weight, "dp", axis=0).reshape(span, held, slab, width)
    out_parts = []
    for step in range(span):
        block = lax.dynamic_index_in_dim(out_rows, place ^ step, 0, keepdims=False)
        out_parts.append(block if step == 0 else swap_bit_any(block, step))
    out_full = unxor(jnp.stack(out_parts, axis=0), place, span)
    out_full = out_full.transpose(1, 0, 2, 3).reshape(cols, width)
    up = up_weight.reshape(slab, groups, size, hidden_slab).transpose(2, 0, 1, 3)
    up = line.exchange(up.reshape(size, slab, groups * hidden_slab))
    up_full = lax.all_gather(up.reshape(size * slab, groups * hidden_slab), "dp", axis=0, tiled=True)
    down_full = lax.all_gather(down_weight, "dp", axis=0, tiled=True)
    grad_full = [line.gather(cotangent[m]) for m in range(micro)]

    input_square = jnp.zeros((), F32)
    branch_square = jnp.zeros((), F32)
    mlp_square = jnp.zeros((), F32)
    normed = []
    heads = []
    probs_all = []
    attended = []
    hidden = []
    for m in range(micro):
        tokens = inputs[m].astype(F32)
        input_square = input_square + jnp.sum(tokens * tokens)
        normal, _ = normalize(tokens_full[m].astype(F32))
        normed_low = (normal * gain_one + bias_one).astype(BF16)
        normed.append(normed_low)
        mixed = mm(normed_low, qkv_full)
        query = ((mixed[:, :cols] + query_shift) * scale).astype(BF16)
        key = mixed[:, cols : 2 * cols].astype(BF16)
        value = (mixed[:, 2 * cols :] + value_shift).astype(BF16)
        ids = line.order(block_ids[m])
        allowed = ids[None, :] <= ids[:, None]
        probs_head = []
        att = []
        for h in range(held):
            cut = slice(h * HEAD, (h + 1) * HEAD)
            scores = jnp.where(allowed, mm_rt(query[:, cut], key[:, cut]), NEGATIVE)
            expo = jnp.exp(scores - jnp.max(scores, axis=-1, keepdims=True))
            probs = expo / jnp.sum(expo, axis=-1, keepdims=True)
            probs_head.append(probs)
            att.append(mm(probs.astype(BF16), value[:, cut]).astype(BF16))
        heads.append((query, key, value))
        probs_all.append(probs_head)
        att = jnp.concatenate(att, axis=1)
        attended.append(att)
        branch = line.scatter(lambda cut: mm(att[cut], out_full)) + out_shift
        branch_square = branch_square + jnp.sum(branch * branch)
        hidden.append(tokens + branch)

    output_rows = []
    normed_two = []
    activation = []
    d_pre_all = []
    d_hidden_all = []
    d_branch_own = []
    gain_two_grad = bias_two_grad = 0.0
    for m in range(micro):
        normal, inverse = normalize(hidden[m])
        normed_two_own = (normal * gain_two + bias_two).astype(BF16)
        n_two = line.gather(normed_two_own)
        normed_two.append(n_two)
        pre = mm(n_two, up_full) + up_shift
        act, slope = gelu_pair(pre)
        act = act.astype(BF16)
        activation.append(act)
        d_pre = (mm_rt(grad_full[m], down_full) * slope).astype(BF16)
        d_pre_all.append(d_pre)
        d_normed_two = line.scatter(lambda cut: mm_rt(d_pre[cut], up_full))
        gain_two_grad = gain_two_grad + jnp.sum(d_normed_two * normal, axis=0)
        bias_two_grad = bias_two_grad + jnp.sum(d_normed_two, axis=0)
        d_hidden = cotangent[m].astype(F32) + normalize_back(normal, inverse, d_normed_two * gain_two)
        d_hidden_all.append(d_hidden)
        d_branch_own.append(d_hidden.astype(BF16))
        branch_two = line.scatter(lambda cut: mm(act[cut], down_full)) + down_shift
        output = hidden[m] + branch_two
        mlp_square = mlp_square + jnp.sum(output * output)
        output_rows.append(output.astype(BF16))

    activation = jnp.concatenate(activation, axis=0)
    grad_cat = jnp.concatenate(grad_full, axis=0)
    d_pre_cat = jnp.concatenate(d_pre_all, axis=0)
    n_two_cat = jnp.concatenate(normed_two, axis=0)
    down_grad = mm_lt(activation, grad_cat).astype(BF16)
    down_sum = lax.psum_scatter(down_grad, "dp", scatter_dimension=0, tiled=True)
    up_grad = mm_lt(n_two_cat, d_pre_cat).astype(BF16)
    up_sum = lax.psum_scatter(up_grad, "dp", scatter_dimension=0, tiled=True)
    up_sum = line.exchange(up_sum.reshape(size, slab, groups * hidden_slab))
    up_sum = up_sum.reshape(size, slab, groups, hidden_slab).transpose(1, 2, 0, 3).reshape(slab, -1)
    up_bias_grad = jnp.sum(d_pre_cat.astype(F32), axis=0)

    d_branch_full = []
    d_heads = []
    d_normed_own = []
    gain_one_grad = bias_one_grad = 0.0
    for m in range(micro):
        d_branch = line.gather(d_branch_own[m])
        d_branch_full.append(d_branch)
        d_att = mm_rt(d_branch, out_full).astype(BF16)
        query, key, value = heads[m]
        d_query, d_key, d_value = [], [], []
        for h in range(held):
            cut = slice(h * HEAD, (h + 1) * HEAD)
            probs = probs_all[m][h]
            d_probs = mm_rt(d_att[:, cut], value[:, cut])
            delta = jnp.sum(probs * d_probs, axis=-1, keepdims=True)
            d_scores = (probs * (d_probs - delta)).astype(BF16)
            d_query.append(mm(d_scores, key[:, cut]).astype(BF16))
            d_key.append(mm_lt(d_scores, query[:, cut]).astype(BF16))
            d_value.append(mm_lt(probs.astype(BF16), d_att[:, cut]).astype(BF16))
        d_qkv = jnp.concatenate(d_query + d_key + d_value, axis=1)
        d_heads.append(d_qkv)

        def terms(cut, d_qkv=d_qkv):
            return mm_rt(d_qkv[cut, :cols], qkv_full[:, :cols]) * scale + mm_rt(
                d_qkv[cut, cols:], qkv_full[:, cols:]
            )

        whole = terms(slice(None))
        normal, _ = normalize(tokens_full[m].astype(F32))
        gain_one_grad = gain_one_grad + jnp.sum(whole * normal, axis=0)
        bias_one_grad = bias_one_grad + jnp.sum(whole, axis=0)
        d_normed_own.append(line.scatter(lambda cut: whole[cut]))

    d_heads = jnp.concatenate(d_heads, axis=0)
    d_branch_full = jnp.concatenate(d_branch_full, axis=0)
    attended = jnp.concatenate(attended, axis=0)
    normed = jnp.concatenate(normed, axis=0)
    qkv_grad = mm_lt(normed, d_heads)
    qkv_grad = jnp.concatenate([qkv_grad[:, :cols] * scale, qkv_grad[:, cols:]], axis=1).astype(BF16)
    out_grad = mm_lt(attended, d_branch_full).astype(BF16)
    out_grad = out_grad.reshape(held, span, slab, width).transpose(1, 0, 2, 3)
    out_parts = []
    for step in range(span):
        block = lax.dynamic_index_in_dim(out_grad, place ^ step, 0, keepdims=False)
        out_parts.append(block if step == 0 else swap_bit_any(block, step))
    out_grad = unxor(jnp.stack(out_parts, axis=0), place, span).reshape(groups * slab, width)
    out_sum = lax.psum_scatter(out_grad, "dp", scatter_dimension=0, tiled=True)
    qkv_sum = lax.psum_scatter(qkv_grad, "dp", scatter_dimension=0, tiled=True)
    qkv_sum = line.exchange(qkv_sum.reshape(size, slab, 3 * cols))
    qkv_sum = qkv_sum.reshape(bands, span, slab, 3, held, HEAD).transpose(3, 2, 1, 4, 0, 5)
    qkv_sum = qkv_sum.reshape(3, slab, width).astype(F32)

    d_heads_sum = jnp.sum(d_heads.astype(F32), axis=0)
    out_bias_grad = sum(jnp.sum(part.astype(F32), axis=0) for part in d_branch_own)
    down_bias_grad = sum(jnp.sum(cotangent[m].astype(F32), axis=0) for m in range(micro))

    input_rows = []
    for m in range(micro):
        normal, inverse = normalize(inputs[m].astype(F32))
        input_rows.append(
            d_hidden_all[m] + normalize_back(normal, inverse, d_normed_own[m] * gain_one)
        )

    up_bias_whole = jnp.zeros((groups, size, hidden_slab), F32)
    up_bias_whole = lax.dynamic_update_slice(
        up_bias_whole, up_bias_grad.reshape(groups, 1, hidden_slab), (0, own, 0)
    ).reshape(-1)
    scalars = jnp.stack([input_square, branch_square, mlp_square])
    scalars = jnp.concatenate([scalars, jnp.zeros((HEAD - 3,), F32)])
    early = sum_small(
        jnp.concatenate(
            [scalars, down_bias_grad, gain_two_grad, bias_two_grad, out_bias_grad, up_bias_whole]
        )
    )
    late = sum_small(
        jnp.concatenate(
            [
                gain_one_grad,
                bias_one_grad,
                head_place(d_heads_sum[:cols] * scale),
                head_place(d_heads_sum[2 * cols :]),
            ]
        )
    )
    index = dp_own * size + own

    def own_part(whole, start, length):
        return lax.dynamic_slice_in_dim(whole, start + index * length, length, 0)

    rms = jnp.sqrt(early[:3] / (micro * rows * devices * width))
    down_bias_sum, gain_two_sum, bias_two_sum, out_bias_sum = (
        own_part(early, HEAD + i * width, slab) for i in range(4)
    )
    up_bias_sum = own_part(early, HEAD + 4 * width, hidden_slab)
    gain_one_sum, bias_one_sum, query_bias_sum, value_bias_sum = (
        own_part(late, i * width, slab) for i in range(4)
    )
    return (
        jnp.stack(output_rows, axis=0),
        jnp.stack(input_rows, axis=0),
        gain_one_sum,
        bias_one_sum,
        qkv_sum[0],
        query_bias_sum,
        qkv_sum[1],
        qkv_sum[2],
        value_bias_sum,
        out_sum.astype(F32),
        out_bias_sum,
        gain_two_sum,
        bias_two_sum,
        up_sum.astype(F32),
        up_bias_sum,
        down_sum.astype(F32),
        down_bias_sum,
        rms[0],
        rms[1],
        rms[2],
    )


def swap_bit_any(array, step):
    size = lax.axis_size("fsdp")
    return lax.ppermute(array, "fsdp", [(i, i ^ step) for i in range(size)])


def unxor(parts, place, span):
    bit = 1
    while bit < span:
        shape = parts.shape
        split = parts.reshape((span // (2 * bit), 2, bit) + shape[1:])
        split = jnp.where((place & bit) != 0, split[:, ::-1], split)
        parts = split.reshape(shape)
        bit *= 2
    return parts


def solution(mesh):
    shard = P(("dp", "fsdp"))
    matrix = P(("dp", "fsdp"), None)
    rows = P("dp", "fsdp", None)
    in_specs = (
        rows,
        P("dp", None),
        rows,
        shard,
        shard,
        matrix,
        shard,
        matrix,
        matrix,
        shard,
        matrix,
        shard,
        shard,
        shard,
        matrix,
        shard,
        matrix,
        shard,
    )
    out_specs = (
        rows,
        rows,
        shard,
        shard,
        matrix,
        shard,
        matrix,
        matrix,
        shard,
        matrix,
        shard,
        shard,
        shard,
        matrix,
        shard,
        matrix,
        shard,
        P(),
        P(),
        P(),
    )
    return jax.shard_map(local, mesh=mesh, in_specs=in_specs, out_specs=out_specs, check_vma=False)
```

time: 4110 us -> 679 us (0.17)
  waiting for transfers between devices: 3290 us -> 226 us
  matrix products: 492 us -> 91 us
  starting transfers between devices: 3.2 us -> 198 us
  blocking collectives: 124 us -> 0 us
    reduce_scatter x6 -> x4, waiting for transfers between devices: 1890 us -> 0.04 us  [the longest x1 0.02 us: local(): up_sum = lax.psum_scatter(up_grad, 'dp', scatter_dimension=0, tiled=True)]
    unnamed x80 -> x8, waiting for transfers between devices: 778 us -> 0.8 us
    all_gather x10 -> x4, waiting for transfers between devices: 620 us -> 0.06 us  [the longest x1 0.02 us: local(): lax.all_gather(out_weight, 'dp', axis=0).reshape(span, held, slab, width)]
    dot_general x132 -> x52, matrix products: 492 us -> 91 us  [dot(): lax.dot_general(left, right, (dims, ((), ())), preferred_element_type=F32)]
    ppermute x0 -> x113, waiting for transfers between devices: none -> 225 us  [the longest x76 173 us: along_chips(): lax.ppermute(array, 'fsdp', [(2 * a + c, 2 * b + c) for a, b in pairs for...]
    ppermute x0 -> x113, starting transfers between devices: none -> 198 us  [the longest x76 170 us: along_chips(): lax.ppermute(array, 'fsdp', [(2 * a + c, 2 * b + c) for a, b in pairs for...]
    unnamed x2 -> x0, blocking collectives: 84.6 us -> none
    unnamed x704 -> x339, local copies, waits for them, and re-layouts: 102 us -> 43.2 us
  transfers between devices with their start and end apart: 48 -> 121, of which waited for: 42 -> 45; matrix products, arithmetic and copies ran while one was open for 13% -> 29% of each run, Pallas kernels for 0% -> 0%
where the time goes in v1:
time: 679 us; the launch traced here: 670 us
  waiting for transfers between devices  226 us (33%)
  starting transfers between devices  198 us (29%)
  matrix products  91 us (13%)
  local copies, waits for them, and re-layouts  77.9 us (11%)
  other arithmetic  55.4 us (8%)
  between operations  21.8 us (3%)
    ppermute x76, waiting for transfers between devices, along_chips(): lax.ppermute(array, 'fsdp', [(2 * a + c, 2 * b + c) for a, b in pairs for...  173 us
    ppermute x76, starting transfers between devices, along_chips(): lax.ppermute(array, 'fsdp', [(2 * a + c, 2 * b + c) for a, b in pairs for...  170 us
    dot_general x52, matrix products, dot(): lax.dot_general(left, right, (dims, ((), ())), preferred_element_type=F32)  91 us
    ppermute x15, waiting for transfers between devices, swap_bit(): return lax.ppermute(array, axis, [(i, i ^ bit) for i in range(size)])  44.5 us
    unnamed x339, local copies, waits for them, and re-layouts  43.2 us
    ppermute x15, starting transfers between devices, swap_bit(): return lax.ppermute(array, axis, [(i, i ^ bit) for i in range(size)])  23.8 us
  transfers between devices with their start and end apart: 121, of which 45 were waited for; matrix products, arithmetic and copies ran while one was open for 29% of the time, Pallas kernels for 0%

profile of v1, /device:TPU:0, one launch (start us, length us, event | category | flops | bytes accessed | tf_op | source)
XLA Modules:
  0.0 670.1 jit_solution(3047190214517036540)
XLA Ops:
  19.1 4.8 collective-permute-done.12
  26.7 9.0 %collective-permute-done.11 = bf16[2,64,768]{2,1,0:T(8,128)(2,1)S(1)} collective-permute-done((bf16[2,64,768]{2,1,0:T(8,128)(2,1)S(1)}, bf16[2,64,768]{2,1,0:T(8,128)(2,1)S(1)}, u32[]{:S(2)}, u32[]{:S(2)}) %collective-permute-start.11) | collective-permute-done | bytes 196640 | tf_op jit(solution)/shard_map/ppermute | solution.py:56
  43.4 7.8 %collective-permute-done.25 = bf16[2,64,1024]{2,1,0:T(8,128)(2,1)S(1)} collective-permute-done((bf16[2,64,1024]{2,1,0:T(8,128)(2,1)S(1)}, bf16[2,64,1024]{2,1,0:T(8,128)(2,1)S(1)}, u32[]{:S(2)}, u32[]{:S(2)}) %collective-permute-start.25) | collective-permute-done | bytes 262176 | tf_op jit(solution)/shard_map/ppermute | solution.py:56
  51.2 13.4 %collective-permute-done.26 = bf16[2,64,1024]{2,1,0:T(8,128)(2,1)S(1)} collective-permute-done((bf16[2,64,1024]{2,1,0:T(8,128)(2,1)S(1)}, bf16[2,64,1024]{2,1,0:T(8,128)(2,1)S(1)}, u32[]{:S(2)}, u32[]{:S(2)}) %collective-permute-start.26) | collective-permute-done | bytes 262176 | tf_op jit(solution)/shard_map/ppermute | solution.py:56
  78.6 14.1 %collective-permute-done.6 = bf16[2,768]{1,0:T(2,128)(2,1)S(1)} collective-permute-done((bf16[2,768]{1,0:T(2,128)(2,1)S(1)}, bf16[2,768]{1,0:T(2,128)(2,1)S(1)}, u32[]{:S(2)}, u32[]{:S(2)}) %collective-permute-start.6) | collective-permute-done | bytes 3104 | tf_op jit(solution)/shard_map/ppermute | solution.py:134
  92.7 5.6 collective-permute-start.7
  122.4 6.1 collective-permute-start.74
  128.5 7.0 %collective-permute-start.75 = (bf16[64,2048]{1,0:T(8,128)(2,1)}, bf16[64,2048]{1,0:T(8,128)(2,1)}, u32[]{:S(2)}, u32[]{:S(2)}) collective-permute-start(bf16[64,2048]{1,0:T(8,128)(2,1)} %get-tuple-element.170), channel_id=1, source_target_pairs={{0,2},{1,3},{2,4},{3,5},{4,6},{5,7},{6,0},{7,1},{8,10},{9,11},{10,... | collective-permute-start | bytes 786440 | tf_op jit(solution)/shard_map/ppermute | solution.py:56
  144.3 4.6 collective-permute-done.57
  157.9 4.5 fusion.269
  174.2 6.1 collective-permute-start.16
  181.5 4.6 collective-permute-done.16
  186.1 4.4 collective-permute-start.40
  191.3 4.5 collective-permute-done.40
  201.5 6.5 collective-permute-start.41
  210.3 10.1 %collective-permute-done.19 = bf16[64,2048]{1,0:T(8,128)(2,1)S(1)} collective-permute-done((bf16[64,2048]{1,0:T(8,128)(2,1)S(1)}, bf16[64,2048]{1,0:T(8,128)(2,1)S(1)}, u32[]{:S(2)}, u32[]{:S(2)}) %collective-permute-start.19) | collective-permute-done | bytes 262176 | tf_op jit(solution)/shard_map/ppermute | solution.py:56
  220.4 5.6 collective-permute-done.43
  231.5 5.8 collective-permute-done.21
  241.6 7.4 %collective-permute-done.23 = bf16[64,2048]{1,0:T(8,128)(2,1)S(1)} collective-permute-done((bf16[64,2048]{1,0:T(8,128)(2,1)S(1)}, bf16[64,2048]{1,0:T(8,128)(2,1)S(1)}, u32[]{:S(2)}, u32[]{:S(2)}) %collective-permute-start.23) | collective-permute-done | bytes 262176 | tf_op jit(solution)/shard_map/ppermute | solution.py:56
  258.6 11.0 %collective-permute-done.45 = bf16[64,2048]{1,0:T(8,128)(2,1)S(1)} collective-permute-done((bf16[64,2048]{1,0:T(8,128)(2,1)S(1)}, bf16[64,2048]{1,0:T(8,128)(2,1)S(1)}, u32[]{:S(2)}, u32[]{:S(2)}) %collective-permute-start.45) | collective-permute-done | bytes 262176 | tf_op jit(solution)/shard_map/ppermute | solution.py:56
  273.2 7.8 %collective-permute-done.47 = bf16[64,2048]{1,0:T(8,128)(2,1)S(1)} collective-permute-done((bf16[64,2048]{1,0:T(8,128)(2,1)S(1)}, bf16[64,2048]{1,0:T(8,128)(2,1)S(1)}, u32[]{:S(2)}, u32[]{:S(2)}) %collective-permute-start.47) | collective-permute-done | bytes 262176 | tf_op jit(solution)/shard_map/ppermute | solution.py:56
  287.7 5.3 fusion.272
  294.3 4.5 multiply_convert_fusion.1
  298.9 3.7 convolution_convert_fusion.5
  303.2 4.6 fusion.31
  328.3 5.2 collective-permute-start.30
  335.5 5.2 collective-permute-start.60
  341.5 5.3 collective-permute-start.81
  347.1 13.2 %collective-permute-start.31 = (bf16[64,2048]{1,0:T(8,128)(2,1)S(1)}, bf16[64,2048]{1,0:T(8,128)(2,1)S(1)}, u32[]{:S(2)}, u32[]{:S(2)}) collective-permute-start(bf16[64,2048]{1,0:T(8,128)(2,1)S(1)} %get-tuple-element.98), channel_id=1, source_target_pairs={{0,2},{1,3},{2,4},{3,5},{4,6},{5,7},{6,0},{7,1},{8,10},{9,11},{10,... | collective-permute-start | bytes 786440 | tf_op jit(solution)/shard_map/ppermute | solution.py:56
  364.5 6.9 %collective-permute-start.51 = (bf16[64,2048]{1,0:T(8,128)(2,1)S(1)}, bf16[64,2048]{1,0:T(8,128)(2,1)S(1)}, u32[]{:S(2)}, u32[]{:S(2)}) collective-permute-start(bf16[64,2048]{1,0:T(8,128)(2,1)S(1)} %get-tuple-element.100), channel_id=1, source_target_pairs={{0,2},{1,3},{2,4},{3,5},{4,6},{5,7},{6,0},{7,1},{8,10},{9,11},{10,... | collective-permute-start | bytes 786440 | tf_op jit(solution)/shard_map/ppermute | solution.py:56
  371.4 3.9 collective-permute-done.33
  375.4 6.5 collective-permute-done.61
  387.7 5.3 collective-permute-done.51
  395.5 7.0 %collective-permute-start.65 = (bf16[64,2048]{1,0:T(8,128)(2,1)S(1)}, bf16[64,2048]{1,0:T(8,128)(2,1)S(1)}, u32[]{:S(2)}, u32[]{:S(2)}) collective-permute-start(bf16[64,2048]{1,0:T(8,128)(2,1)S(1)} %get-tuple-element.64), channel_id=1, source_target_pairs={{0,2},{1,3},{2,4},{3,5},{4,6},{5,7},{6,0},{7,1},{8,10},{9,11},{10,... | collective-permute-start | bytes 786440 | tf_op jit(solution)/shard_map/ppermute | solution.py:56
  402.5 3.9 collective-permute-done.65
  411.3 3.7 collective-permute-start.84
  415.1 7.8 %collective-permute-start.85 = (bf16[64,2048]{1,0:T(8,128)(2,1)}, bf16[64,2048]{1,0:T(8,128)(2,1)}, u32[]{:S(2)}, u32[]{:S(2)}) collective-permute-start(bf16[64,2048]{1,0:T(8,128)(2,1)} %get-tuple-element.154), channel_id=1, source_target_pairs={{0,2},{1,3},{2,4},{3,5},{4,6},{5,7},{6,0},{7,1},{8,10},{9,11},{10,... | collective-permute-start | bytes 786440 | tf_op jit(solution)/shard_map/ppermute | solution.py:56
  428.3 8.4 %convolution_convert_fusion.1 = bf16[2048,1024]{1,0:T(8,128)(2,1)} fusion(bf16[1024,2048]{1,0:T(8,128)(2,1)} %get-tuple-element.121, bf16[512,1024]{1,0:T(8,128)(2,1)S(1)} %fusion.31, bf16[512,1024]{1,0:T(8,128)(2,1)S(1)} %fusion.25), kind=kOutput, calls=%fused_computation.29 | convolution fusion | flops 4301258752 | bytes 10485760 | tf_op jit(solution)/shard_map/dot_general | solution.py:16
  502.0 4.5 collective-permute-done.105
  507.9 4.6 collective-permute-start.107
  512.5 9.5 %convolution_convert_fusion = bf16[1024,2048]{1,0:T(8,128)(2,1)} fusion(bf16[1024,2048]{1,0:T(8,128)(2,1)} %copy-done.103, bf16[512,1024]{1,0:T(8,128)(2,1)} %get-tuple-element.229, bf16[512,1024]{1,0:T(8,128)(2,1)} %get-tuple-element.228), kind=kOutput, calls=%fused_computation.28 | convolution fusion | flops 4301258752 | bytes 10485760 | tf_op jit(solution)/shard_map/dot_general | solution.py:16
  546.5 3.9 collective-permute-start.70
  557.2 4.1 collective-permute-start.71
  563.5 10.4 %collective-permute-start.91 = (bf16[64,2048]{1,0:T(8,128)(2,1)S(1)}, bf16[64,2048]{1,0:T(8,128)(2,1)S(1)}, u32[]{:S(2)}, u32[]{:S(2)}) collective-permute-start(bf16[64,2048]{1,0:T(8,128)(2,1)S(1)} %get-tuple-element.90), channel_id=1, source_target_pairs={{0,2},{1,3},{2,4},{3,5},{4,6},{5,7},{6,0},{7,1},{8,10},{9,11},{10,... | collective-permute-start | bytes 786440 | tf_op jit(solution)/shard_map/ppermute | solution.py:56
  577.3 12.9 %collective-permute-done.98 = f32[8192]{0:T(1024)S(1)} collective-permute-done((f32[8192]{0:T(1024)S(1)}, f32[8192]{0:T(1024)S(1)}, u32[]{:S(2)}, u32[]{:S(2)}) %collective-permute-start.98) | collective-permute-done | bytes 32800 | tf_op jit(solution)/shard_map/ppermute | solution.py:134
  596.3 5.9 collective-permute-done.109
  602.1 14.6 %collective-permute-done.110 = bf16[2,64,1024]{2,1,0:T(8,128)(2,1)S(1)} collective-permute-done((bf16[2,64,1024]{2,1,0:T(8,128)(2,1)S(1)}, bf16[2,64,1024]{2,1,0:T(8,128)(2,1)S(1)}, u32[]{:S(2)}, u32[]{:S(2)}) %collective-permute-start.110) | collective-permute-done | bytes 262176 | tf_op jit(solution)/shard_map/ppermute | solution.py:56
  626.9 13.2 %collective-permute-done.100 = bf16[2,64,768]{2,1,0:T(8,128)(2,1)S(1)} collective-permute-done((bf16[2,64,768]{2,1,0:T(8,128)(2,1)S(1)}, bf16[2,64,768]{2,1,0:T(8,128)(2,1)S(1)}, u32[]{:S(2)}, u32[]{:S(2)}) %collective-permute-start.100) | collective-permute-done | bytes 196640 | tf_op jit(solution)/shard_map/ppermute | solution.py:56
  (803 shorter events, 313.5 us)
Async XLA Ops:
  7.2 145.3 %all-gather.12.cloned.1.call-start = ((), (), s32[]{:S(2)}) async-start(), calls=%async_computation.11 | async-start | bytes 1310720 | tf_op jit(solution)/shard_map/all_gather | solution.py:227
  7.9 150.0 %all-gather.6.cloned.1.call-start = ((), (), s32[]{:S(2)}) async-start(), calls=%async_computation.4 | async-start | bytes 3932160 | tf_op jit(solution)/shard_map/all_gather | solution.py:225
  18.2 17.5 %collective-permute-start.11 = (bf16[2,64,768]{2,1,0:T(8,128)(2,1)S(1)}, bf16[2,64,768]{2,1,0:T(8,128)(2,1)S(1)}, u32[]{:S(2)}, u32[]{:S(2)}) collective-permute-start(bf16[2,64,768]{2,1,0:T(8,128)(2,1)S(1)} %get-tuple-element.150), channel_id=1, source_target_pairs={{0,4},{1,5},{2,6},{3,7},{4,0},{5,1},{6,2},{7,3},{8,12},{9,13},{10,... | collective-permute-start | bytes 589832 | tf_op jit(solution)/shard_map/ppermute | solution.py:56
  39.1 248.6 %all-gather.8.cloned.1.call-start = ((), (), s32[]{:S(2)}) async-start(), calls=%async_computation.5 | async-start | bytes 5242880 | tf_op jit(solution)/shard_map/all_gather | solution.py:236
  42.7 21.8 %collective-permute-start.26 = (bf16[2,64,1024]{2,1,0:T(8,128)(2,1)S(1)}, bf16[2,64,1024]{2,1,0:T(8,128)(2,1)S(1)}, u32[]{:S(2)}, u32[]{:S(2)}) collective-permute-start(bf16[2,64,1024]{2,1,0:T(8,128)(2,1)S(1)} %get-tuple-element.136), channel_id=1, source_target_pairs={{0,4},{1,5},{2,6},{3,7},{4,0},{5,1},{6,2},{7,3},{8,12},{9,13},{10,... | collective-permute-start | bytes 786440 | tf_op jit(solution)/shard_map/ppermute | solution.py:56
  42.7 21.8 %collective-permute-start.27 = (bf16[2,64,1024]{2,1,0:T(8,128)(2,1)S(1)}, bf16[2,64,1024]{2,1,0:T(8,128)(2,1)S(1)}, u32[]{:S(2)}, u32[]{:S(2)}) collective-permute-start(bf16[2,64,1024]{2,1,0:T(8,128)(2,1)S(1)} %get-tuple-element.138), channel_id=1, source_target_pairs={{0,2},{1,3},{2,4},{3,5},{4,6},{5,7},{6,0},{7,1},{8,10},{9,11},{10,... | collective-permute-start | bytes 786440 | tf_op jit(solution)/shard_map/ppermute | solution.py:56
  68.4 230.5 %all-gather.10.cloned.1.call-start = ((), (), s32[]{:S(2)}) async-start(), calls=%async_computation.6 | async-start | bytes 5242880 | tf_op jit(solution)/shard_map/all_gather | solution.py:237
  69.3 49.9 %collective-permute-start = (bf16[64,2048]{1,0:T(8,128)(2,1)}, bf16[64,2048]{1,0:T(8,128)(2,1)S(1)}, u32[]{:S(2)}, u32[]{:S(2)}) collective-permute-start(bf16[64,2048]{1,0:T(8,128)(2,1)} %get-tuple-element.171), channel_id=1, source_target_pairs={{0,6},{1,7},{2,0},{3,1},{4,2},{5,3},{6,4},{7,5},{8,14},{9,15},{10,... | collective-permute-start | bytes 786440 | tf_op jit(solution)/shard_map/ppermute | solution.py:56
  69.3 49.2 %collective-permute-start.1 = (bf16[64,2048]{1,0:T(8,128)(2,1)}, bf16[64,2048]{1,0:T(8,128)(2,1)S(1)}, u32[]{:S(2)}, u32[]{:S(2)}) collective-permute-start(bf16[64,2048]{1,0:T(8,128)(2,1)} %get-tuple-element.171), channel_id=1, source_target_pairs={{0,2},{1,3},{2,4},{3,5},{4,6},{5,7},{6,0},{7,1},{8,10},{9,11},{10,... | collective-permute-start | bytes 786440 | tf_op jit(solution)/shard_map/ppermute | solution.py:56
  71.3 41.5 %collective-permute-start.34 = (bf16[64,2048]{1,0:T(8,128)(2,1)}, bf16[64,2048]{1,0:T(8,128)(2,1)}, u32[]{:S(2)}, u32[]{:S(2)}) collective-permute-start(bf16[64,2048]{1,0:T(8,128)(2,1)} %get-tuple-element.172), channel_id=1, source_target_pairs={{0,6},{1,7},{2,0},{3,1},{4,2},{5,3},{6,4},{7,5},{8,14},{9,15},{10,... | collective-permute-start | bytes 786440 | tf_op jit(solution)/shard_map/ppermute | solution.py:56
  74.2 46.2 %collective-permute-start.35 = (bf16[64,2048]{1,0:T(8,128)(2,1)}, bf16[64,2048]{1,0:T(8,128)(2,1)S(1)}, u32[]{:S(2)}, u32[]{:S(2)}) collective-permute-start(bf16[64,2048]{1,0:T(8,128)(2,1)} %get-tuple-element.172), channel_id=1, source_target_pairs={{0,2},{1,3},{2,4},{3,5},{4,6},{5,7},{6,0},{7,1},{8,10},{9,11},{10,... | collective-permute-start | bytes 786440 | tf_op jit(solution)/shard_map/ppermute | solution.py:56
  74.5 517.8 %reduce-scatter.9.cloned.1.call-start = ((), (), s32[]{:S(2)}) async-start(), calls=%async_computation.9 | async-start | bytes 5242880 | tf_op jit(solution)/shard_map/reduce_scatter | solution.py:313
  117.2 23.2 %collective-permute-start.37 = (bf16[64,2048]{1,0:T(8,128)(2,1)}, bf16[64,2048]{1,0:T(8,128)(2,1)S(1)}, u32[]{:S(2)}, u32[]{:S(2)}) collective-permute-start(bf16[64,2048]{1,0:T(8,128)(2,1)} %collective-permute-done.34), channel_id=1, source_target_pairs={{2,0},{3,1},{4,2},{5,3},{10,8},{11,9},{12,10},{13,11},{18,16},{19,... | collective-permute-start | bytes 786440 | tf_op jit(solution)/shard_map/ppermute | solution.py:56
  119.2 18.8 %collective-permute-start.3 = (bf16[64,2048]{1,0:T(8,128)(2,1)S(1)}, bf16[64,2048]{1,0:T(8,128)(2,1)S(1)}, u32[]{:S(2)}, u32[]{:S(2)}) collective-permute-start(bf16[64,2048]{1,0:T(8,128)(2,1)S(1)} %collective-permute-done), channel_id=1, source_target_pairs={{2,0},{3,1},{4,2},{5,3},{10,8},{11,9},{12,10},{13,11},{18,16},{19,... | collective-permute-start | bytes 786440 | tf_op jit(solution)/shard_map/ppermute | solution.py:56
  120.5 18.8 %collective-permute-start.36 = (bf16[64,2048]{1,0:T(8,128)(2,1)S(1)}, bf16[64,2048]{1,0:T(8,128)(2,1)S(1)}, u32[]{:S(2)}, u32[]{:S(2)}) collective-permute-start(bf16[64,2048]{1,0:T(8,128)(2,1)S(1)} %collective-permute-done.35), channel_id=1, source_target_pairs={{2,4},{3,5},{4,6},{5,7},{10,12},{11,13},{12,14},{13,15},{18,20},{1... | collective-permute-start | bytes 786440 | tf_op jit(solution)/shard_map/ppermute | solution.py:56
  122.4 79.1 %collective-permute-start.74 = (bf16[64,2048]{1,0:T(8,128)(2,1)}, bf16[64,2048]{1,0:T(8,128)(2,1)}, u32[]{:S(2)}, u32[]{:S(2)}) collective-permute-start(bf16[64,2048]{1,0:T(8,128)(2,1)} %get-tuple-element.170), channel_id=1, source_target_pairs={{0,6},{1,7},{2,0},{3,1},{4,2},{5,3},{6,4},{7,5},{8,14},{9,15},{10,... | collective-permute-start | bytes 786440 | tf_op jit(solution)/shard_map/ppermute | solution.py:56
  128.5 79.7 %collective-permute-start.75 = (bf16[64,2048]{1,0:T(8,128)(2,1)}, bf16[64,2048]{1,0:T(8,128)(2,1)}, u32[]{:S(2)}, u32[]{:S(2)}) collective-permute-start(bf16[64,2048]{1,0:T(8,128)(2,1)} %get-tuple-element.170), channel_id=1, source_target_pairs={{0,2},{1,3},{2,4},{3,5},{4,6},{5,7},{6,0},{7,1},{8,10},{9,11},{10,... | collective-permute-start | bytes 786440 | tf_op jit(solution)/shard_map/ppermute | solution.py:56
  172.2 35.8 %collective-permute-start.58 = (bf16[256,2048]{1,0:T(8,128)(2,1)S(1)}, bf16[256,2048]{1,0:T(8,128)(2,1)S(1)}, u32[]{:S(2)}, u32[]{:S(2)}) collective-permute-start(bf16[256,2048]{1,0:T(8,128)(2,1)S(1)} %pad_maximum_fusion.10), channel_id=1, source_target_pairs={{0,1},{1,0},{2,3},{3,2},{4,5},{5,4},{6,7},{7,6},{8,9},{9,8},{10,11... | collective-permute-start | bytes 3145736 | tf_op jit(solution)/shard_map/ppermute | solution.py:52
  198.3 22.0 %collective-permute-start.19 = (bf16[64,2048]{1,0:T(8,128)(2,1)S(1)}, bf16[64,2048]{1,0:T(8,128)(2,1)S(1)}, u32[]{:S(2)}, u32[]{:S(2)}) collective-permute-start(bf16[64,2048]{1,0:T(8,128)(2,1)S(1)} %get-tuple-element.103), channel_id=1, source_target_pairs={{0,6},{1,7},{2,0},{3,1},{4,2},{5,3},{6,4},{7,5},{8,14},{9,15},{10,... | collective-permute-start | bytes 786440 | tf_op jit(solution)/shard_map/ppermute | solution.py:56
  201.5 18.8 %collective-permute-start.41 = (bf16[64,2048]{1,0:T(8,128)(2,1)S(1)}, bf16[64,2048]{1,0:T(8,128)(2,1)S(1)}, u32[]{:S(2)}, u32[]{:S(2)}) collective-permute-start(bf16[64,2048]{1,0:T(8,128)(2,1)S(1)} %get-tuple-element.104), channel_id=1, source_target_pairs={{0,2},{1,3},{2,4},{3,5},{4,6},{5,7},{6,0},{7,1},{8,10},{9,11},{10,... | collective-permute-start | bytes 786440 | tf_op jit(solution)/shard_map/ppermute | solution.py:56
  208.0 18.0 %collective-permute-start.43 = (bf16[64,2048]{1,0:T(8,128)(2,1)S(1)}, bf16[64,2048]{1,0:T(8,128)(2,1)S(1)}, u32[]{:S(2)}, u32[]{:S(2)}) collective-permute-start(bf16[64,2048]{1,0:T(8,128)(2,1)S(1)} %get-tuple-element.105), channel_id=1, source_target_pairs={{0,6},{1,7},{2,0},{3,1},{4,2},{5,3},{6,4},{7,5},{8,14},{9,15},{10,... | collective-permute-start | bytes 786440 | tf_op jit(solution)/shard_map/ppermute | solution.py:56
  208.3 49.0 %collective-permute-start.76 = (bf16[64,2048]{1,0:T(8,128)(2,1)}, bf16[64,2048]{1,0:T(8,128)(2,1)S(1)}, u32[]{:S(2)}, u32[]{:S(2)}) collective-permute-start(bf16[64,2048]{1,0:T(8,128)(2,1)} %collective-permute-done.75), channel_id=1, source_target_pairs={{2,4},{3,5},{4,6},{5,7},{10,12},{11,13},{12,14},{13,15},{18,20},{1... | collective-permute-start | bytes 786440 | tf_op jit(solution)/shard_map/ppermute | solution.py:56
  209.0 48.3 %collective-permute-start.77 = (bf16[64,2048]{1,0:T(8,128)(2,1)}, bf16[64,2048]{1,0:T(8,128)(2,1)S(1)}, u32[]{:S(2)}, u32[]{:S(2)}) collective-permute-start(bf16[64,2048]{1,0:T(8,128)(2,1)} %collective-permute-done.74), channel_id=1, source_target_pairs={{2,0},{3,1},{4,2},{5,3},{10,8},{11,9},{12,10},{13,11},{18,16},{19,... | collective-permute-start | bytes 786440 | tf_op jit(solution)/shard_map/ppermute | solution.py:56
  258.6 24.4 %collective-permute-start.78 = (bf16[256,2048]{1,0:T(8,128)(2,1)S(1)}, bf16[256,2048]{1,0:T(8,128)(2,1)S(1)}, u32[]{:S(2)}, u32[]{:S(2)}) collective-permute-start(bf16[256,2048]{1,0:T(8,128)(2,1)S(1)} %pad_maximum_fusion.12), channel_id=1, source_target_pairs={{0,1},{1,0},{2,3},{3,2},{4,5},{5,4},{6,7},{7,6},{8,9},{9,8},{10,11... | collective-permute-start | bytes 3145736 | tf_op jit(solution)/shard_map/ppermute | solution.py:52
  317.7 42.7 %collective-permute-start.50 = (bf16[64,2048]{1,0:T(8,128)(2,1)S(1)}, bf16[64,2048]{1,0:T(8,128)(2,1)S(1)}, u32[]{:S(2)}, u32[]{:S(2)}) collective-permute-start(bf16[64,2048]{1,0:T(8,128)(2,1)S(1)} %slice.952), channel_id=1, source_target_pairs={{0,2},{1,3},{2,4},{3,5},{8,10},{9,11},{10,12},{11,13},{16,18},{17,... | collective-permute-start | bytes 786440 | tf_op jit(solution)/shard_map/ppermute | solution.py:56
  321.3 39.2 %collective-permute-start.52 = (bf16[64,2048]{1,0:T(8,128)(2,1)S(1)}, bf16[64,2048]{1,0:T(8,128)(2,1)S(1)}, u32[]{:S(2)}, u32[]{:S(2)}) collective-permute-start(bf16[64,2048]{1,0:T(8,128)(2,1)S(1)} %slice.952), channel_id=1, source_target_pairs={{4,2},{5,3},{6,4},{7,5},{12,10},{13,11},{14,12},{15,13},{20,18},{2... | collective-permute-start | bytes 786440 | tf_op jit(solution)/shard_map/ppermute | solution.py:56
  341.5 21.0 %collective-permute-start.81 = (bf16[64,2048]{1,0:T(8,128)(2,1)S(1)}, bf16[64,2048]{1,0:T(8,128)(2,1)S(1)}, u32[]{:S(2)}, u32[]{:S(2)}) collective-permute-start(bf16[64,2048]{1,0:T(8,128)(2,1)S(1)} %get-tuple-element.96), channel_id=1, source_target_pairs={{0,2},{1,3},{2,4},{3,5},{4,6},{5,7},{6,0},{7,1},{8,10},{9,11},{10,... | collective-permute-start | bytes 786440 | tf_op jit(solution)/shard_map/ppermute | solution.py:56
  347.0 17.5 %collective-permute-start.83 = (bf16[64,2048]{1,0:T(8,128)(2,1)S(1)}, bf16[64,2048]{1,0:T(8,128)(2,1)S(1)}, u32[]{:S(2)}, u32[]{:S(2)}) collective-permute-start(bf16[64,2048]{1,0:T(8,128)(2,1)S(1)} %get-tuple-element.97), channel_id=1, source_target_pairs={{0,6},{1,7},{2,0},{3,1},{4,2},{5,3},{6,4},{7,5},{8,14},{9,15},{10,... | collective-permute-start | bytes 786440 | tf_op jit(solution)/shard_map/ppermute | solution.py:56
  347.1 24.3 %collective-permute-start.31 = (bf16[64,2048]{1,0:T(8,128)(2,1)S(1)}, bf16[64,2048]{1,0:T(8,128)(2,1)S(1)}, u32[]{:S(2)}, u32[]{:S(2)}) collective-permute-start(bf16[64,2048]{1,0:T(8,128)(2,1)S(1)} %get-tuple-element.98), channel_id=1, source_target_pairs={{0,2},{1,3},{2,4},{3,5},{4,6},{5,7},{6,0},{7,1},{8,10},{9,11},{10,... | collective-permute-start | bytes 786440 | tf_op jit(solution)/shard_map/ppermute | solution.py:56
  360.5 21.3 %collective-permute-start.61 = (bf16[64,2048]{1,0:T(8,128)(2,1)S(1)}, bf16[64,2048]{1,0:T(8,128)(2,1)S(1)}, u32[]{:S(2)}, u32[]{:S(2)}) collective-permute-start(bf16[64,2048]{1,0:T(8,128)(2,1)S(1)} %get-tuple-element.94), channel_id=1, source_target_pairs={{0,2},{1,3},{2,4},{3,5},{4,6},{5,7},{6,0},{7,1},{8,10},{9,11},{10,... | collective-permute-start | bytes 786440 | tf_op jit(solution)/shard_map/ppermute | solution.py:56
  362.5 23.0 %collective-permute-start.63 = (bf16[64,2048]{1,0:T(8,128)(2,1)S(1)}, bf16[64,2048]{1,0:T(8,128)(2,1)S(1)}, u32[]{:S(2)}, u32[]{:S(2)}) collective-permute-start(bf16[64,2048]{1,0:T(8,128)(2,1)S(1)} %get-tuple-element.95), channel_id=1, source_target_pairs={{0,6},{1,7},{2,0},{3,1},{4,2},{5,3},{6,4},{7,5},{8,14},{9,15},{10,... | collective-permute-start | bytes 786440 | tf_op jit(solution)/shard_map/ppermute | solution.py:56
  364.5 28.6 %collective-permute-start.51 = (bf16[64,2048]{1,0:T(8,128)(2,1)S(1)}, bf16[64,2048]{1,0:T(8,128)(2,1)S(1)}, u32[]{:S(2)}, u32[]{:S(2)}) collective-permute-start(bf16[64,2048]{1,0:T(8,128)(2,1)S(1)} %get-tuple-element.100), channel_id=1, source_target_pairs={{0,2},{1,3},{2,4},{3,5},{4,6},{5,7},{6,0},{7,1},{8,10},{9,11},{10,... | collective-permute-start | bytes 786440 | tf_op jit(solution)/shard_map/ppermute | solution.py:56
  371.4 21.6 %collective-permute-start.53 = (bf16[64,2048]{1,0:T(8,128)(2,1)S(1)}, bf16[64,2048]{1,0:T(8,128)(2,1)S(1)}, u32[]{:S(2)}, u32[]{:S(2)}) collective-permute-start(bf16[64,2048]{1,0:T(8,128)(2,1)S(1)} %get-tuple-element.101), channel_id=1, source_target_pairs={{0,6},{1,7},{2,0},{3,1},{4,2},{5,3},{6,4},{7,5},{8,14},{9,15},{10,... | collective-permute-start | bytes 786440 | tf_op jit(solution)/shard_map/ppermute | solution.py:56
  411.3 26.1 %collective-permute-start.84 = (bf16[64,2048]{1,0:T(8,128)(2,1)}, bf16[64,2048]{1,0:T(8,128)(2,1)}, u32[]{:S(2)}, u32[]{:S(2)}) collective-permute-start(bf16[64,2048]{1,0:T(8,128)(2,1)} %get-tuple-element.154), channel_id=1, source_target_pairs={{0,6},{1,7},{2,0},{3,1},{4,2},{5,3},{6,4},{7,5},{8,14},{9,15},{10,... | collective-permute-start | bytes 786440 | tf_op jit(solution)/shard_map/ppermute | solution.py:56
  415.1 21.7 %collective-permute-start.85 = (bf16[64,2048]{1,0:T(8,128)(2,1)}, bf16[64,2048]{1,0:T(8,128)(2,1)}, u32[]{:S(2)}, u32[]{:S(2)}) collective-permute-start(bf16[64,2048]{1,0:T(8,128)(2,1)} %get-tuple-element.154), channel_id=1, source_target_pairs={{0,2},{1,3},{2,4},{3,5},{4,6},{5,7},{6,0},{7,1},{8,10},{9,11},{10,... | collective-permute-start | bytes 786440 | tf_op jit(solution)/shard_map/ppermute | solution.py:56
  436.7 181.1 %reduce-scatter.5.cloned.1.call-start = ((), (), s32[]{:S(2)}) async-start(), calls=%async_computation.7 | async-start | bytes 3932160 | tf_op jit(solution)/shard_map/reduce_scatter | solution.py:365
  481.9 160.2 %reduce-scatter.7.cloned.1.call-start = ((), (), s32[]{:S(2)}) async-start(), calls=%async_computation.8 | async-start | bytes 1310720 | tf_op jit(solution)/shard_map/reduce_scatter | solution.py:364
  489.9 154.0 %reduce-scatter.11.cloned.1.call-start = ((), (), s32[]{:S(2)}) async-start(), calls=%async_computation.10 | async-start | bytes 5242880 | tf_op jit(solution)/shard_map/reduce_scatter | solution.py:311
  522.0 18.3 %collective-permute-start.108 = (f32[16512]{0:T(1024)S(1)}, f32[16512]{0:T(1024)S(1)}, u32[]{:S(2)}, u32[]{:S(2)}) collective-permute-start(f32[16512]{0:T(1024)S(1)} %add.612), channel_id=1, source_target_pairs={{0,4},{1,5},{2,6},{3,7},{4,0},{5,1},{6,2},{7,3},{8,12},{9,13},{10,... | collective-permute-start | bytes 198152 | tf_op jit(solution)/shard_map/ppermute | solution.py:134
  551.1 23.3 %collective-permute-start.97 = (f32[8192]{0:T(1024)S(1)}, f32[8192]{0:T(1024)S(1)}, u32[]{:S(2)}, u32[]{:S(2)}) collective-permute-start(f32[8192]{0:T(1024)S(1)} %add.594), channel_id=1, source_target_pairs={{0,2},{1,3},{2,0},{3,1},{4,6},{5,7},{6,4},{7,5},{8,10},{9,11},{10,... | collective-permute-start | bytes 98312 | tf_op jit(solution)/shard_map/ppermute | solution.py:134
  557.2 33.7 %collective-permute-start.71 = (bf16[64,2048]{1,0:T(8,128)(2,1)S(1)}, bf16[64,2048]{1,0:T(8,128)(2,1)S(1)}, u32[]{:S(2)}, u32[]{:S(2)}) collective-permute-start(bf16[64,2048]{1,0:T(8,128)(2,1)S(1)} %get-tuple-element.92), channel_id=1, source_target_pairs={{0,2},{1,3},{2,4},{3,5},{4,6},{5,7},{6,0},{7,1},{8,10},{9,11},{10,... | collective-permute-start | bytes 786440 | tf_op jit(solution)/shard_map/ppermute | solution.py:56
  561.3 29.5 %collective-permute-start.73 = (bf16[64,2048]{1,0:T(8,128)(2,1)S(1)}, bf16[64,2048]{1,0:T(8,128)(2,1)S(1)}, u32[]{:S(2)}, u32[]{:S(2)}) collective-permute-start(bf16[64,2048]{1,0:T(8,128)(2,1)S(1)} %get-tuple-element.93), channel_id=1, source_target_pairs={{0,6},{1,7},{2,0},{3,1},{4,2},{5,3},{6,4},{7,5},{8,14},{9,15},{10,... | collective-permute-start | bytes 786440 | tf_op jit(solution)/shard_map/ppermute | solution.py:56
  563.5 27.3 %collective-permute-start.91 = (bf16[64,2048]{1,0:T(8,128)(2,1)S(1)}, bf16[64,2048]{1,0:T(8,128)(2,1)S(1)}, u32[]{:S(2)}, u32[]{:S(2)}) collective-permute-start(bf16[64,2048]{1,0:T(8,128)(2,1)S(1)} %get-tuple-element.90), channel_id=1, source_target_pairs={{0,2},{1,3},{2,4},{3,5},{4,6},{5,7},{6,0},{7,1},{8,10},{9,11},{10,... | collective-permute-start | bytes 786440 | tf_op jit(solution)/shard_map/ppermute | solution.py:56
  594.3 22.4 %collective-permute-start.110 = (bf16[2,64,1024]{2,1,0:T(8,128)(2,1)S(1)}, bf16[2,64,1024]{2,1,0:T(8,128)(2,1)S(1)}, u32[]{:S(2)}, u32[]{:S(2)}) collective-permute-start(bf16[2,64,1024]{2,1,0:T(8,128)(2,1)S(1)} %get-tuple-element.118), channel_id=1, source_target_pairs={{0,4},{1,5},{2,6},{3,7},{4,0},{5,1},{6,2},{7,3},{8,12},{9,13},{10,... | collective-permute-start | bytes 786440 | tf_op jit(solution)/shard_map/ppermute | solution.py:56
  595.1 21.6 %collective-permute-start.111 = (bf16[2,64,1024]{2,1,0:T(8,128)(2,1)S(1)}, bf16[2,64,1024]{2,1,0:T(8,128)(2,1)S(1)}, u32[]{:S(2)}, u32[]{:S(2)}) collective-permute-start(bf16[2,64,1024]{2,1,0:T(8,128)(2,1)S(1)} %get-tuple-element.120), channel_id=1, source_target_pairs={{0,2},{1,3},{2,4},{3,5},{4,6},{5,7},{6,0},{7,1},{8,10},{9,11},{10,... | collective-permute-start | bytes 786440 | tf_op jit(solution)/shard_map/ppermute | solution.py:56
  617.7 29.0 %collective-permute-start.112 = (bf16[4,64,1024]{2,1,0:T(8,128)(2,1)}, bf16[4,64,1024]{2,1,0:T(8,128)(2,1)}, u32[]{:S(2)}, u32[]{:S(2)}) collective-permute-start(bf16[4,64,1024]{2,1,0:T(8,128)(2,1)} %get-tuple-element.116), channel_id=1, source_target_pairs={{0,1},{1,0},{2,3},{3,2},{4,5},{5,4},{6,7},{7,6},{8,9},{9,8},{10,11... | collective-permute-start | bytes 1572872 | tf_op jit(solution)/shard_map/ppermute | solution.py:52
  619.7 20.4 %collective-permute-start.100 = (bf16[2,64,768]{2,1,0:T(8,128)(2,1)S(1)}, bf16[2,64,768]{2,1,0:T(8,128)(2,1)S(1)}, u32[]{:S(2)}, u32[]{:S(2)}) collective-permute-start(bf16[2,64,768]{2,1,0:T(8,128)(2,1)S(1)} %get-tuple-element.144), channel_id=1, source_target_pairs={{0,4},{1,5},{2,6},{3,7},{4,0},{5,1},{6,2},{7,3},{8,12},{9,13},{10,... | collective-permute-start | bytes 589832 | tf_op jit(solution)/shard_map/ppermute | solution.py:56
  622.2 17.9 %collective-permute-start.101 = (bf16[2,64,768]{2,1,0:T(8,128)(2,1)S(1)}, bf16[2,64,768]{2,1,0:T(8,128)(2,1)S(1)}, u32[]{:S(2)}, u32[]{:S(2)}) collective-permute-start(bf16[2,64,768]{2,1,0:T(8,128)(2,1)S(1)} %get-tuple-element.146), channel_id=1, source_target_pairs={{0,2},{1,3},{2,4},{3,5},{4,6},{5,7},{6,0},{7,1},{8,10},{9,11},{10,... | collective-permute-start | bytes 589832 | tf_op jit(solution)/shard_map/ppermute | solution.py:56
  (226 other events, 2071.0 us)
Sparse Core Ops, SparseCore 0:
  9.9 29.3 all-gather.11
  41.1 43.9 all-gather.5
  87.5 53.2 all-gather.7
  142.5 52.6 all-gather.9
  436.8 52.3 reduce-scatter.8
  492.3 44.5 reduce-scatter.4
  540.7 27.7 reduce-scatter.6
  571.4 52.6 reduce-scatter.10
